TPU v7x, 512 devices: a whole 4x8x8 slice. The times are simulated.
512 devices in a mesh: section: 32 (over x, y), expert: 4 (over z_hi), dp: 4 (over z_lo, core).
Axes of the slice: x: 4, y: 8, z: 8 (z_hi: 4, z_lo: 2; z = z_hi * 2 + z_lo), core: 2. Of those that a mesh axis runs over, the one named last changes fastest.
Arguments:
- state_in: bfloat16 [2, 32, 256, 3584], P(None, 'section', 'dp', 'expert'), may hold values from -1.5 to 1.5
- saved_inputs: bfloat16 [4, 2, 32, 256, 3584], P(None, None, 'section', 'dp', 'expert'), may hold values from -6 to 6
- slot_rows: int32 [4, 2, 32, 256], P(None, None, 'section', 'dp'), may hold values from 0 to 63, as said below
- combine: float32 [4, 2, 32, 256], P(None, None, 'section', 'dp'), may hold values from 0.4 to 0.7
- w_gate: bfloat16 [32, 3584, 1024], P('section', 'expert', 'dp'), may hold values from -0.09375 to 0.09375
- w_up: bfloat16 [32, 3584, 1024], P('section', 'expert', 'dp'), may hold values from -0.125 to 0.125
- w_down: bfloat16 [32, 1024, 3584], P('section', 'dp', 'expert'), may hold values from -0.25 to 0.25
Outputs:
- state_out: bfloat16 [2, 32, 256, 3584], P(None, 'section', 'dp', 'expert')
- grad_gate: bfloat16 [32, 3584, 1024], P('section', 'expert', 'dp')
- grad_up: bfloat16 [32, 3584, 1024], P('section', 'expert', 'dp')
Inputs may be any that keep to these rules, and one draw needn't show every extreme that they name: `slot_rows`: each aligned block of 64 slots holds every one of the 64 token rows of the block's group once, counted from the group's first token.
All inputs are finite; a program needn't handle non-finite values.
Results may differ from a plain program's by a relative error of at most 0.035.
Values may be sent and summed in bfloat16 or wider, within the bound.
A program may use at most 64 MiB of HBM per device.

v0:
```python
import jax
import jax.numpy as jnp
from jax import lax
from jax.sharding import PartitionSpec as P


def for_sending(array):
    return jax.tree.map(lambda a: a.astype(jnp.bfloat16) if a.dtype == jnp.float32 else a, array)


def from_behind(array, axis, by):
    length = lax.axis_size(axis)
    return lax.ppermute(array, axis, [(i, (i + by) % length) for i in range(length)])


def silu_grads(pre_gate, pre_up, hidden_grad):
    sigmoid_gate = jax.nn.sigmoid(pre_gate)
    gate_grad = (
        hidden_grad * pre_up * sigmoid_gate * (1.0 + pre_gate * (1.0 - sigmoid_gate))
    ).astype(jnp.bfloat16)
    up_grad = (hidden_grad * pre_gate * sigmoid_gate).astype(jnp.bfloat16)
    return (gate_grad, up_grad)


def width_sums(inputs, slot_grads, gate_w, up_w, down_w):
    pre_gate = jnp.dot(inputs, gate_w, preferred_element_type=jnp.float32)
    pre_up = jnp.dot(inputs, up_w, preferred_element_type=jnp.float32)
    hidden_grad = lax.dot_general(
        slot_grads, down_w, (((1,), (1,)), ((), ())), preferred_element_type=jnp.float32
    )
    return (
        lax.psum(pre_gate.astype(jnp.bfloat16), "expert").astype(jnp.float32),
        lax.psum(pre_up.astype(jnp.bfloat16), "expert").astype(jnp.float32),
        lax.psum(hidden_grad.astype(jnp.bfloat16), "expert").astype(jnp.float32),
    )


def on_device(state_in, saved_inputs, slot_rows, combine, w_gate, w_up, w_down):
    gate_w = w_gate[0]
    up_w = w_up[0]
    down_w = w_down[0]
    groups = lax.axis_size("dp")
    slot_count = saved_inputs.shape[3]
    step_count = saved_inputs.shape[0]

    def section_layer(grads_state, inputs, slot_index, weights):
        picked = grads_state[slot_index]
        slot_grads = (weights[:, None] * picked.astype(jnp.float32)).astype(jnp.bfloat16)
        all_inputs, all_grads = (
            lax.all_gather(inputs, "dp", axis=0, tiled=True),
            lax.all_gather(slot_grads, "dp", axis=0, tiled=True),
        )
        pre_gate, pre_up, hidden_grad = width_sums(all_inputs, all_grads, gate_w, up_w, down_w)
        gate_grad, up_grad = silu_grads(pre_gate, pre_up, hidden_grad)
        contract = (((1,), (1,)), ((), ()))
        first = lax.dot_general(gate_grad, gate_w, contract, preferred_element_type=jnp.float32)
        added_grad = lax.psum_scatter(
            (
                first + lax.dot_general(up_grad, up_w, contract, preferred_element_type=jnp.float32)
            ).astype(jnp.bfloat16),
            "dp",
            scatter_dimension=0,
            tiled=True,
        ).astype(jnp.float32)
        retained = (all_inputs, gate_grad, up_grad)
        updated = (picked.astype(jnp.float32) + added_grad).astype(jnp.bfloat16)
        return (grads_state.at[slot_index].set(updated), retained)

    def advance(step_index, states):
        fresh_states = []
        retained_parts = []
        for direction in range(2):
            fresh, retained = section_layer(
                states[direction],
                saved_inputs[step_index, direction, 0],
                slot_rows[step_index, direction, 0],
                combine[step_index, direction, 0],
            )
            fresh_states.append(fresh)
            retained_parts.append(retained)
        stacked = tuple(
            (jnp.stack([retained_parts[0][place], retained_parts[1][place]]) for place in range(3))
        )
        return (jnp.stack(fresh_states), stacked)

    def scan_step(states, step_index):
        states, retained = advance(step_index, states)
        moved_down = from_behind(for_sending(states[0]), "section", -1)
        moved_up = from_behind(for_sending(states[1]), "section", 1)
        return (jnp.stack([moved_down, moved_up]), retained)

    states, looped = lax.scan(scan_step, state_in[:, 0], jnp.arange(step_count - 1))
    states, closing = advance(step_count - 1, states)
    inputs_all, gate_all, up_all = tuple(
        (jnp.concatenate([looped[place], closing[place][None]], axis=0) for place in range(3))
    )
    inputs_g = inputs_all.reshape(step_count, 2, groups, slot_count, inputs_all.shape[-1])
    gate_g = gate_all.reshape(step_count, 2, groups, slot_count, gate_all.shape[-1])
    up_g = up_all.reshape(step_count, 2, groups, slot_count, up_all.shape[-1])
    per_gate = jnp.einsum("tcgsd,tcgsh->gdh", inputs_g, gate_g, preferred_element_type=jnp.float32)
    per_up = jnp.einsum("tcgsd,tcgsh->gdh", inputs_g, up_g, preferred_element_type=jnp.float32)
    narrow_gate = lax.optimization_barrier(per_gate.astype(jnp.bfloat16))
    narrow_up = lax.optimization_barrier(per_up.astype(jnp.bfloat16))
    grad_gate = jnp.sum(narrow_gate.astype(jnp.float32), axis=0)
    grad_up = jnp.sum(narrow_up.astype(jnp.float32), axis=0)
    return (
        states[:, None],
        grad_gate.astype(jnp.bfloat16)[None],
        grad_up.astype(jnp.bfloat16)[None],
    )


def solution(mesh):
    placed = (
        P(None, "section", "dp", "expert"),
        P(None, None, "section", "dp", "expert"),
        P(None, None, "section", "dp"),
        P(None, None, "section", "dp"),
        P("section", "expert", "dp"),
        P("section", "expert", "dp"),
        P("section", "dp", "expert"),
    )
    return jax.shard_map(
        on_device,
        mesh=mesh,
        in_specs=placed,
        out_specs=(
            P(None, "section", "dp", "expert"),
            P("section", "expert", "dp"),
            P("section", "expert", "dp"),
        ),
        check_vma=False,
    )
```

profile of v0, /device:TPU:1, one launch (start us, length us, event | category | flops | bytes accessed | tf_op | source)
XLA Modules:
  0.0 681.7 jit_solution(15119023042480068632)
XLA Ops:
  9.1 13.2 %all-gather.3 = bf16[1,1,1,256,896]{4,3,2,1,0:T(8,128)(2,1)S(1)} all-gather(bf16[1,1,1,64,896]{4,3,2,1,0:T(8,128)(2,1)S(1)} %get-tuple-element.129), channel_id=5, replica_groups=mesh['section'=32,'expert'=4,'dp'=4] {'dp'}, dimensions={3}, use_global_device_ids=true | all-gather | bytes 573440 | tf_op jit(solution)/shard_map/all_gather | solution.py:50
  22.3 2.1 convolution_convert_fusion.6
  24.5 2.0 convolution_convert_fusion.7
  26.4 6.9 %all-gather.2 = bf16[1,1,1,256,896]{4,3,2,1,0:T(8,128)(2,1)S(1)} all-gather(bf16[1,1,1,64,896]{4,3,2,1,0:T(8,128)(2,1)S(1)} %get-tuple-element.128), channel_id=4, replica_groups=mesh['section'=32,'expert'=4,'dp'=4] {'dp'}, dimensions={3}, use_global_device_ids=true | all-gather | bytes 573440 | tf_op jit(solution)/shard_map/all_gather | solution.py:50
  35.3 502.4 %while.16 = (s32[]{:T(128)}, bf16[2,64,896]{2,1,0:T(8,128)(2,1)S(1)}, bf16[3,2,256,896]{3,2,1,0:T(8,128)(2,1)}, bf16[3,2,256,256]{3,2,1,0:T(8,128)(2,1)}, bf16[3...) while((s32[]{:T(128)}, ...), condition=%wide.region_11.12_spmd, body=%wide.region_0.11_spmd.sunk | while | flops 1183058304 | bytes 33632240 | solution.py:92
  38.9 6.9 %all-gather.6 = bf16[1,1,1,256,896]{4,3,2,1,0:T(8,128)(2,1)S(1)} all-gather(bf16[1,1,1,64,896]{4,3,2,1,0:T(8,128)(2,1)S(1)} %get-tuple-element.238), channel_id=3, replica_groups=mesh['section'=32,'expert'=4,'dp'=4] {'dp'}, dimensions={3}, use_global_device_ids=true | all-gather | bytes 573440 | tf_op jit(solution)/shard_map/while/body/eval_jaxpr/all_gather | solution.py:50
  47.7 6.9 %all-gather.7 = bf16[1,1,1,256,896]{4,3,2,1,0:T(8,128)(2,1)S(1)} all-gather(bf16[1,1,1,64,896]{4,3,2,1,0:T(8,128)(2,1)S(1)} %get-tuple-element.242), channel_id=2, replica_groups=mesh['section'=32,'expert'=4,'dp'=4] {'dp'}, dimensions={3}, use_global_device_ids=true | all-gather | bytes 573440 | tf_op jit(solution)/shard_map/while/body/eval_jaxpr/all_gather | solution.py:50
  57.4 6.9 %all_gather.30 = bf16[256,896]{1,0:T(8,128)(2,1)S(1)} all-gather(bf16[64,896]{1,0:T(8,128)(2,1)S(1)} %fusion.189), channel_id=1, replica_groups=mesh['section'=32,'expert'=4,'dp'=4] {'dp'}, dimensions={0}, use_global_device_ids=true | all-gather | bytes 573440 | tf_op jit(solution)/shard_map/while/body/eval_jaxpr/all_gather | solution.py:51
  65.2 6.9 %all_gather.31 = bf16[256,896]{1,0:T(8,128)(2,1)S(1)} all-gather(bf16[64,896]{1,0:T(8,128)(2,1)S(1)} %fusion.190), channel_id=1, replica_groups=mesh['section'=32,'expert'=4,'dp'=4] {'dp'}, dimensions={0}, use_global_device_ids=true | all-gather | bytes 573440 | tf_op jit(solution)/shard_map/while/body/eval_jaxpr/all_gather | solution.py:51
  74.2 66.6 %all-reduce.9.cloned.1.call-done = (bf16[256,256]{1,0:T(8,128)(2,1)}, bf16[256,256]{1,0:T(8,128)(2,1)}, bf16[256,256]{1,0:T(8,128)(2,1)}, bf16[256,256]{1,0:T(8,...) async-done(((bf16[256,256]{1,0:T(8,128)(2,1)}, bf16[256,256]{1,0:T(8,128)(2,1)}, bf16[256,256]{1,0:T(8,128)(2,1)}, bf16[256,256]{1,0:T(8,128)(2,1)}, ...) | async-done | bytes 786448 | tf_op jit(solution)/shard_map/while/body/eval_jaxpr/psum | solution.py:34
  140.8 1.2 fusion.191
  142.3 2.1 fusion.193
  144.5 1.7 fusion.194
  148.7 17.6 %reduce-scatter.9.cloned.1.call-done = bf16[64,896]{1,0:T(8,128)(2,1)} async-done(((bf16[256,896]{1,0:T(8,128)(2,1)}), bf16[64,896]{1,0:T(8,128)(2,1)}) %reduce-scatter.9.cloned.1.call-update) | async-done | bytes 114704 | tf_op jit(solution)/shard_map/while/body/eval_jaxpr/reduce_scatter | solution.py:57
  166.3 1.3 scatter_custom_fusion.14
  167.6 3.2 collective-permute-start
  170.8 22.4 %reduce-scatter.11.cloned.1.call-done = bf16[64,896]{1,0:T(8,128)(2,1)} async-done(((bf16[256,896]{1,0:T(8,128)(2,1)}), bf16[64,896]{1,0:T(8,128)(2,1)}) %reduce-scatter.11.cloned.1.call-update) | async-done | bytes 114704 | tf_op jit(solution)/shard_map/while/body/eval_jaxpr/reduce_scatter | solution.py:57
  193.2 1.3 scatter_custom_fusion.15
  194.5 6.6 collective-permute-start.1
  201.9 1.6 collective-permute-done.1
  207.2 7.0 %all-gather.6 = bf16[1,1,1,256,896]{4,3,2,1,0:T(8,128)(2,1)S(1)} all-gather(bf16[1,1,1,64,896]{4,3,2,1,0:T(8,128)(2,1)S(1)} %get-tuple-element.238), channel_id=3, replica_groups=mesh['section'=32,'expert'=4,'dp'=4] {'dp'}, dimensions={3}, use_global_device_ids=true | all-gather | bytes 573440 | tf_op jit(solution)/shard_map/while/body/eval_jaxpr/all_gather | solution.py:50
  216.1 6.9 %all-gather.7 = bf16[1,1,1,256,896]{4,3,2,1,0:T(8,128)(2,1)S(1)} all-gather(bf16[1,1,1,64,896]{4,3,2,1,0:T(8,128)(2,1)S(1)} %get-tuple-element.242), channel_id=2, replica_groups=mesh['section'=32,'expert'=4,'dp'=4] {'dp'}, dimensions={3}, use_global_device_ids=true | all-gather | bytes 573440 | tf_op jit(solution)/shard_map/while/body/eval_jaxpr/all_gather | solution.py:50
  225.8 6.9 %all_gather.30 = bf16[256,896]{1,0:T(8,128)(2,1)S(1)} all-gather(bf16[64,896]{1,0:T(8,128)(2,1)S(1)} %fusion.189), channel_id=1, replica_groups=mesh['section'=32,'expert'=4,'dp'=4] {'dp'}, dimensions={0}, use_global_device_ids=true | all-gather | bytes 573440 | tf_op jit(solution)/shard_map/while/body/eval_jaxpr/all_gather | solution.py:51
  233.6 6.9 %all_gather.31 = bf16[256,896]{1,0:T(8,128)(2,1)S(1)} all-gather(bf16[64,896]{1,0:T(8,128)(2,1)S(1)} %fusion.190), channel_id=1, replica_groups=mesh['section'=32,'expert'=4,'dp'=4] {'dp'}, dimensions={0}, use_global_device_ids=true | all-gather | bytes 573440 | tf_op jit(solution)/shard_map/while/body/eval_jaxpr/all_gather | solution.py:51
  242.5 65.4 %all-reduce.9.cloned.1.call-done = (bf16[256,256]{1,0:T(8,128)(2,1)}, bf16[256,256]{1,0:T(8,128)(2,1)}, bf16[256,256]{1,0:T(8,128)(2,1)}, bf16[256,256]{1,0:T(8,...) async-done(((bf16[256,256]{1,0:T(8,128)(2,1)}, bf16[256,256]{1,0:T(8,128)(2,1)}, bf16[256,256]{1,0:T(8,128)(2,1)}, bf16[256,256]{1,0:T(8,128)(2,1)}, ...) | async-done | bytes 786448 | tf_op jit(solution)/shard_map/while/body/eval_jaxpr/psum | solution.py:34
  308.0 1.2 fusion.191
  309.5 2.1 fusion.193
  311.7 1.7 fusion.194
  315.9 17.5 %reduce-scatter.9.cloned.1.call-done = bf16[64,896]{1,0:T(8,128)(2,1)} async-done(((bf16[256,896]{1,0:T(8,128)(2,1)}), bf16[64,896]{1,0:T(8,128)(2,1)}) %reduce-scatter.9.cloned.1.call-update) | async-done | bytes 114704 | tf_op jit(solution)/shard_map/while/body/eval_jaxpr/reduce_scatter | solution.py:57
  333.5 1.3 scatter_custom_fusion.14
  334.7 3.2 collective-permute-start
  338.0 22.2 %reduce-scatter.11.cloned.1.call-done = bf16[64,896]{1,0:T(8,128)(2,1)} async-done(((bf16[256,896]{1,0:T(8,128)(2,1)}), bf16[64,896]{1,0:T(8,128)(2,1)}) %reduce-scatter.11.cloned.1.call-update) | async-done | bytes 114704 | tf_op jit(solution)/shard_map/while/body/eval_jaxpr/reduce_scatter | solution.py:57
  360.1 1.3 scatter_custom_fusion.15
  361.4 6.7 collective-permute-start.1
  369.0 1.6 collective-permute-done.1
  374.2 7.0 %all-gather.6 = bf16[1,1,1,256,896]{4,3,2,1,0:T(8,128)(2,1)S(1)} all-gather(bf16[1,1,1,64,896]{4,3,2,1,0:T(8,128)(2,1)S(1)} %get-tuple-element.238), channel_id=3, replica_groups=mesh['section'=32,'expert'=4,'dp'=4] {'dp'}, dimensions={3}, use_global_device_ids=true | all-gather | bytes 573440 | tf_op jit(solution)/shard_map/while/body/eval_jaxpr/all_gather | solution.py:50
  383.1 6.9 %all-gather.7 = bf16[1,1,1,256,896]{4,3,2,1,0:T(8,128)(2,1)S(1)} all-gather(bf16[1,1,1,64,896]{4,3,2,1,0:T(8,128)(2,1)S(1)} %get-tuple-element.242), channel_id=2, replica_groups=mesh['section'=32,'expert'=4,'dp'=4] {'dp'}, dimensions={3}, use_global_device_ids=true | all-gather | bytes 573440 | tf_op jit(solution)/shard_map/while/body/eval_jaxpr/all_gather | solution.py:50
  392.8 6.9 %all_gather.30 = bf16[256,896]{1,0:T(8,128)(2,1)S(1)} all-gather(bf16[64,896]{1,0:T(8,128)(2,1)S(1)} %fusion.189), channel_id=1, replica_groups=mesh['section'=32,'expert'=4,'dp'=4] {'dp'}, dimensions={0}, use_global_device_ids=true | all-gather | bytes 573440 | tf_op jit(solution)/shard_map/while/body/eval_jaxpr/all_gather | solution.py:51
  400.6 6.9 %all_gather.31 = bf16[256,896]{1,0:T(8,128)(2,1)S(1)} all-gather(bf16[64,896]{1,0:T(8,128)(2,1)S(1)} %fusion.190), channel_id=1, replica_groups=mesh['section'=32,'expert'=4,'dp'=4] {'dp'}, dimensions={0}, use_global_device_ids=true | all-gather | bytes 573440 | tf_op jit(solution)/shard_map/while/body/eval_jaxpr/all_gather | solution.py:51
  409.6 65.4 %all-reduce.9.cloned.1.call-done = (bf16[256,256]{1,0:T(8,128)(2,1)}, bf16[256,256]{1,0:T(8,128)(2,1)}, bf16[256,256]{1,0:T(8,128)(2,1)}, bf16[256,256]{1,0:T(8,...) async-done(((bf16[256,256]{1,0:T(8,128)(2,1)}, bf16[256,256]{1,0:T(8,128)(2,1)}, bf16[256,256]{1,0:T(8,128)(2,1)}, bf16[256,256]{1,0:T(8,128)(2,1)}, ...) | async-done | bytes 786448 | tf_op jit(solution)/shard_map/while/body/eval_jaxpr/psum | solution.py:34
  474.9 1.2 fusion.191
  476.5 2.1 fusion.193
  478.7 1.7 fusion.194
  482.9 17.6 %reduce-scatter.9.cloned.1.call-done = bf16[64,896]{1,0:T(8,128)(2,1)} async-done(((bf16[256,896]{1,0:T(8,128)(2,1)}), bf16[64,896]{1,0:T(8,128)(2,1)}) %reduce-scatter.9.cloned.1.call-update) | async-done | bytes 114704 | tf_op jit(solution)/shard_map/while/body/eval_jaxpr/reduce_scatter | solution.py:57
  500.4 1.3 scatter_custom_fusion.14
  501.7 3.2 collective-permute-start
  504.9 22.4 %reduce-scatter.11.cloned.1.call-done = bf16[64,896]{1,0:T(8,128)(2,1)} async-done(((bf16[256,896]{1,0:T(8,128)(2,1)}), bf16[64,896]{1,0:T(8,128)(2,1)}) %reduce-scatter.11.cloned.1.call-update) | async-done | bytes 114704 | tf_op jit(solution)/shard_map/while/body/eval_jaxpr/reduce_scatter | solution.py:57
  527.3 1.3 scatter_custom_fusion.15
  528.6 6.6 collective-permute-start.1
  536.1 1.6 collective-permute-done.1
  538.6 7.0 %all_gather.26 = bf16[256,896]{1,0:T(8,128)(2,1)S(1)} all-gather(bf16[64,896]{1,0:T(8,128)(2,1)S(1)} %fusion.81), channel_id=1, replica_groups=mesh['section'=32,'expert'=4,'dp'=4] {'dp'}, dimensions={0}, use_global_device_ids=true | all-gather | bytes 573440 | tf_op jit(solution)/shard_map/all_gather | solution.py:51
  547.5 6.9 %all_gather.24 = bf16[256,896]{1,0:T(8,128)(2,1)S(1)} all-gather(bf16[64,896]{1,0:T(8,128)(2,1)S(1)} %fusion.79), channel_id=1, replica_groups=mesh['section'=32,'expert'=4,'dp'=4] {'dp'}, dimensions={0}, use_global_device_ids=true | all-gather | bytes 573440 | tf_op jit(solution)/shard_map/all_gather | solution.py:51
  555.5 65.4 %all-reduce.7.cloned.1.call-done = (bf16[256,256]{1,0:T(8,128)(2,1)}, bf16[256,256]{1,0:T(8,128)(2,1)}, bf16[256,256]{1,0:T(8,128)(2,1)}, bf16[256,256]{1,0:T(8,...) async-done(((bf16[256,256]{1,0:T(8,128)(2,1)}, bf16[256,256]{1,0:T(8,128)(2,1)}, bf16[256,256]{1,0:T(8,128)(2,1)}, bf16[256,256]{1,0:T(8,128)(2,1)}, ...) | async-done | bytes 786448 | tf_op jit(solution)/shard_map/psum | solution.py:34
  620.8 1.2 fusion.78
  622.4 1.2 fusion.54
  623.8 3.4 maximum_maximum_fusion
  628.9 3.8 bitcast_convert_fusion.1
  632.7 2.7 bitcast_convert_fusion
  635.4 1.1 reduce_sum.24
  636.6 2.7 reduce_sum.25
  639.3 6.3 reduce-scatter.7.cloned.1.call-done
  645.6 1.3 scatter_custom_fusion.3
  646.8 25.5 %reduce-scatter.5.cloned.1.call-done = bf16[64,896]{1,0:T(8,128)(2,1)} async-done(((bf16[256,896]{1,0:T(8,128)(2,1)}), bf16[64,896]{1,0:T(8,128)(2,1)}) %reduce-scatter.5.cloned.1.call-update) | async-done | bytes 114704 | tf_op jit(solution)/shard_map/reduce_scatter | solution.py:57
  672.3 1.3 scatter_custom_fusion.2
  (174 shorter events, 48.2 us)
Async XLA Ops:
  8.0 25.4 %copy-start = (bf16[1,896,256]{2,1,0:T(8,128)(2,1)S(1)}, bf16[1,896,256]{2,1,0:T(8,128)(2,1)}, u32[]{:S(2)}) copy-start(bf16[1,896,256]{2,1,0:T(8,128)(2,1)} %param.13) | copy-start | bytes 1376260
  8.0 26.3 %copy-start.1 = (bf16[1,896,256]{2,1,0:T(8,128)(2,1)S(1)}, bf16[1,896,256]{2,1,0:T(8,128)(2,1)}, u32[]{:S(2)}) copy-start(bf16[1,896,256]{2,1,0:T(8,128)(2,1)} %param.14) | copy-start | bytes 1376260
  9.1 26.2 %copy-start.19 = (s32[4,2,1,64]{3,2,1,0:T(1,128)S(1)}, s32[4,2,1,64]{3,2,1,0:T(1,128)}, u32[]{:S(2)}) copy-start(s32[4,2,1,64]{3,2,1,0:T(1,128)} %param.11) | copy-start | bytes 6148
  9.1 26.2 %copy-start.20 = (f32[4,2,1,64]{3,2,1,0:T(1,128)S(1)}, f32[4,2,1,64]{3,2,1,0:T(1,128)}, u32[]{:S(2)}) copy-start(f32[4,2,1,64]{3,2,1,0:T(1,128)} %param.12) | copy-start | bytes 6148
  9.1 26.2 %copy-start.2 = (bf16[1,256,896]{2,1,0:T(8,128)(2,1)S(1)}, bf16[1,256,896]{2,1,0:T(8,128)(2,1)}, u32[]{:S(2)}) copy-start(bf16[1,256,896]{2,1,0:T(8,128)(2,1)} %param.15) | copy-start | bytes 1376260
  9.1 26.2 %copy-start.6 = (bf16[2,1,64,896]{3,2,1,0:T(8,128)(2,1)S(1)}, bf16[2,1,64,896]{3,2,1,0:T(8,128)(2,1)}, u32[]{:S(2)}) copy-start(bf16[2,1,64,896]{3,2,1,0:T(8,128)(2,1)} %param.9) | copy-start | bytes 688132
  22.3 13.0 %copy-start.7 = (bf16[1,1,1,256,896]{4,3,2,1,0:T(8,128)(2,1)}, bf16[1,1,1,256,896]{4,3,2,1,0:T(8,128)(2,1)S(1)}, u32[]{:S(2)}) copy-start(bf16[1,1,1,256,896]{4,3,2,1,0:T(8,128)(2,1)S(1)} %all-gather.3) | copy-start | bytes 1376260
  33.3 2.0 copy-start.9
  35.3 105.5 %all-reduce.9.cloned.1.call-start = ((), (), s32[]{:S(2)}) async-start(), calls=%async_computation.7 | async-start | bytes 1572864 | tf_op jit(solution)/shard_map/while/body/eval_jaxpr/psum | solution.py:34
  74.1 92.1 %reduce-scatter.9.cloned.1.call-start = ((), (), s32[]{:S(2)}) async-start(), calls=%async_computation.8 | async-start | bytes 573440 | tf_op jit(solution)/shard_map/while/body/eval_jaxpr/reduce_scatter | solution.py:57
  140.8 3.7 copy-start.3
  140.8 3.7 copy-start.4
  144.5 48.7 %reduce-scatter.11.cloned.1.call-start = ((), (), s32[]{:S(2)}) async-start(), calls=%async_computation.9 | async-start | bytes 573440 | tf_op jit(solution)/shard_map/while/body/eval_jaxpr/reduce_scatter | solution.py:57
  147.7 53.4 %copy-start.5 = (bf16[1,256,256]{2,1,0:T(8,128)(2,1)S(1)}, bf16[1,256,256]{2,1,0:T(8,128)(2,1)}, u32[]{:S(2)}) copy-start(bf16[1,256,256]{2,1,0:T(8,128)(2,1)} %get-tuple-element.252) | copy-start | bytes 393220 | tf_op jit(solution)/shard_map/while
  167.6 34.4 %collective-permute-start = (bf16[64,896]{1,0:T(8,128)(2,1)S(1)}, bf16[64,896]{1,0:T(8,128)(2,1)S(1)}, u32[]{:S(2)}, u32[]{:S(2)}) collective-permute-start(bf16[64,896]{1,0:T(8,128)(2,1)S(1)} %scatter_custom_fusion.14), channel_id=1, source_target_pairs={{0,16},{16,32},{32,48},{48,64},{64,80},{80,96},{96,112},{112,128},... | collective-permute-start | bytes 344072 | tf_op jit(solution)/shard_map/while/body/eval_jaxpr/ppermute | solution.py:13
  194.5 9.1 %collective-permute-start.1 = (bf16[64,896]{1,0:T(8,128)(2,1)S(1)}, bf16[64,896]{1,0:T(8,128)(2,1)S(1)}, u32[]{:S(2)}, u32[]{:S(2)}) collective-permute-start(bf16[64,896]{1,0:T(8,128)(2,1)S(1)} %scatter_custom_fusion.15), channel_id=1, source_target_pairs={{0,496},{16,0},{32,16},{48,32},{64,48},{80,64},{96,80},{112,96},{1... | collective-permute-start | bytes 344072 | tf_op jit(solution)/shard_map/while/body/eval_jaxpr/ppermute | solution.py:13
  203.6 104.4 %all-reduce.9.cloned.1.call-start = ((), (), s32[]{:S(2)}) async-start(), calls=%async_computation.7 | async-start | bytes 1572864 | tf_op jit(solution)/shard_map/while/body/eval_jaxpr/psum | solution.py:34
  242.5 91.0 %reduce-scatter.9.cloned.1.call-start = ((), (), s32[]{:S(2)}) async-start(), calls=%async_computation.8 | async-start | bytes 573440 | tf_op jit(solution)/shard_map/while/body/eval_jaxpr/reduce_scatter | solution.py:57
  308.0 3.7 copy-start.3
  308.0 3.7 copy-start.4
  311.6 48.5 %reduce-scatter.11.cloned.1.call-start = ((), (), s32[]{:S(2)}) async-start(), calls=%async_computation.9 | async-start | bytes 573440 | tf_op jit(solution)/shard_map/while/body/eval_jaxpr/reduce_scatter | solution.py:57
  314.8 53.3 %copy-start.5 = (bf16[1,256,256]{2,1,0:T(8,128)(2,1)S(1)}, bf16[1,256,256]{2,1,0:T(8,128)(2,1)}, u32[]{:S(2)}) copy-start(bf16[1,256,256]{2,1,0:T(8,128)(2,1)} %get-tuple-element.252) | copy-start | bytes 393220 | tf_op jit(solution)/shard_map/while
  334.7 34.2 %collective-permute-start = (bf16[64,896]{1,0:T(8,128)(2,1)S(1)}, bf16[64,896]{1,0:T(8,128)(2,1)S(1)}, u32[]{:S(2)}, u32[]{:S(2)}) collective-permute-start(bf16[64,896]{1,0:T(8,128)(2,1)S(1)} %scatter_custom_fusion.14), channel_id=1, source_target_pairs={{0,16},{16,32},{32,48},{48,64},{64,80},{80,96},{96,112},{112,128},... | collective-permute-start | bytes 344072 | tf_op jit(solution)/shard_map/while/body/eval_jaxpr/ppermute | solution.py:13
  361.4 9.2 %collective-permute-start.1 = (bf16[64,896]{1,0:T(8,128)(2,1)S(1)}, bf16[64,896]{1,0:T(8,128)(2,1)S(1)}, u32[]{:S(2)}, u32[]{:S(2)}) collective-permute-start(bf16[64,896]{1,0:T(8,128)(2,1)S(1)} %scatter_custom_fusion.15), channel_id=1, source_target_pairs={{0,496},{16,0},{32,16},{48,32},{64,48},{80,64},{96,80},{112,96},{1... | collective-permute-start | bytes 344072 | tf_op jit(solution)/shard_map/while/body/eval_jaxpr/ppermute | solution.py:13
  370.6 104.3 %all-reduce.9.cloned.1.call-start = ((), (), s32[]{:S(2)}) async-start(), calls=%async_computation.7 | async-start | bytes 1572864 | tf_op jit(solution)/shard_map/while/body/eval_jaxpr/psum | solution.py:34
  409.5 90.9 %reduce-scatter.9.cloned.1.call-start = ((), (), s32[]{:S(2)}) async-start(), calls=%async_computation.8 | async-start | bytes 573440 | tf_op jit(solution)/shard_map/while/body/eval_jaxpr/reduce_scatter | solution.py:57
  474.9 3.7 copy-start.3
  474.9 3.7 copy-start.4
  478.6 48.7 %reduce-scatter.11.cloned.1.call-start = ((), (), s32[]{:S(2)}) async-start(), calls=%async_computation.9 | async-start | bytes 573440 | tf_op jit(solution)/shard_map/while/body/eval_jaxpr/reduce_scatter | solution.py:57
  481.8 53.4 %copy-start.5 = (bf16[1,256,256]{2,1,0:T(8,128)(2,1)S(1)}, bf16[1,256,256]{2,1,0:T(8,128)(2,1)}, u32[]{:S(2)}) copy-start(bf16[1,256,256]{2,1,0:T(8,128)(2,1)} %get-tuple-element.252) | copy-start | bytes 393220 | tf_op jit(solution)/shard_map/while
  501.7 34.4 %collective-permute-start = (bf16[64,896]{1,0:T(8,128)(2,1)S(1)}, bf16[64,896]{1,0:T(8,128)(2,1)S(1)}, u32[]{:S(2)}, u32[]{:S(2)}) collective-permute-start(bf16[64,896]{1,0:T(8,128)(2,1)S(1)} %scatter_custom_fusion.14), channel_id=1, source_target_pairs={{0,16},{16,32},{32,48},{48,64},{64,80},{80,96},{96,112},{112,128},... | collective-permute-start | bytes 344072 | tf_op jit(solution)/shard_map/while/body/eval_jaxpr/ppermute | solution.py:13
  528.6 9.1 %collective-permute-start.1 = (bf16[64,896]{1,0:T(8,128)(2,1)S(1)}, bf16[64,896]{1,0:T(8,128)(2,1)S(1)}, u32[]{:S(2)}, u32[]{:S(2)}) collective-permute-start(bf16[64,896]{1,0:T(8,128)(2,1)S(1)} %scatter_custom_fusion.15), channel_id=1, source_target_pairs={{0,496},{16,0},{32,16},{48,32},{64,48},{80,64},{96,80},{112,96},{1... | collective-permute-start | bytes 344072 | tf_op jit(solution)/shard_map/while/body/eval_jaxpr/ppermute | solution.py:13
  537.7 83.1 %all-reduce.7.cloned.1.call-start = ((), (), s32[]{:S(2)}) async-start(), calls=%async_computation.6 | async-start | bytes 1572864 | tf_op jit(solution)/shard_map/psum | solution.py:34
  555.4 68.4 %copy-start.8 = (bf16[1,1,1,256,896]{4,3,2,1,0:T(8,128)(2,1)S(1)}, bf16[1,1,1,256,896]{4,3,2,1,0:T(8,128)(2,1)}, u32[]{:S(2)}) copy-start(bf16[1,1,1,256,896]{4,3,2,1,0:T(8,128)(2,1)} %copy-done.7) | copy-start | bytes 1376260
  555.4 68.4 %copy-start.10 = (bf16[1,1,1,256,896]{4,3,2,1,0:T(8,128)(2,1)S(1)}, bf16[1,1,1,256,896]{4,3,2,1,0:T(8,128)(2,1)}, u32[]{:S(2)}) copy-start(bf16[1,1,1,256,896]{4,3,2,1,0:T(8,128)(2,1)} %copy-done.9) | copy-start | bytes 1376260
  555.4 90.1 %reduce-scatter.7.cloned.1.call-start = ((), (), s32[]{:S(2)}) async-start(), calls=%async_computation.5 | async-start | bytes 573440 | tf_op jit(solution)/shard_map/reduce_scatter | solution.py:57
  622.0 5.2 copy-start.12
  623.5 48.8 %reduce-scatter.5.cloned.1.call-start = ((), (), s32[]{:S(2)}) async-start(), calls=%async_computation.4 | async-start | bytes 573440 | tf_op jit(solution)/shard_map/reduce_scatter | solution.py:57
  623.8 3.4 copy-start.16
  623.8 3.4 copy-start.17
  623.8 3.4 copy-start.18
  627.4 1.5 copy-start.14
  628.9 3.8 copy-start.11
  628.9 3.8 copy-start.13
  628.9 3.8 copy-start.15
  628.9 3.8 copy-start.21
Sparse Core Ops, SparseCore 0:
  74.2 66.5 all-reduce.8
  144.6 21.6 reduce-scatter.8
  169.3 23.7 reduce-scatter.10
  242.6 65.3 all-reduce.8
  311.8 21.6 reduce-scatter.8
  336.4 23.7 reduce-scatter.10
  409.6 65.2 all-reduce.8
  478.7 21.6 reduce-scatter.8
  503.5 23.7 reduce-scatter.10
Sparse Core Ops, SparseCore 1:
  555.5 65.3 all-reduce.6
  623.6 21.9 reduce-scatter.6
  648.5 23.8 reduce-scatter.4
where the time goes:
time: 683 us; the launch traced here: 682 us
  waiting for transfers between devices  419 us (61%)
  blocking collectives  117 us (17%)
  matrix products  46.2 us (7%)
  other arithmetic  34.6 us (5%)
  starting transfers between devices  30.3 us (4%)
  between operations  15.7 us (2%)
  local copies, waits for them, and re-layouts  11.7 us (2%)
    psum x4, waiting for transfers between devices, width_sums(): lax.psum(hidden_grad.astype(jnp.bfloat16), 'expert').astype(jnp.float32)  263 us
    reduce_scatter x8, waiting for transfers between devices, section_layer(): lax.psum_scatter((first + lax.dot_general(up_grad, up_w, contract, prefer...  151 us
    all_gather x8, blocking collectives, section_layer(): lax.all_gather(inputs, 'dp', axis=0, tiled=True)  61.8 us
    all_gather x8, blocking collectives, section_layer(): lax.all_gather(slot_grads, 'dp', axis=0, tiled=True)  55.6 us
    ppermute x6, starting transfers between devices, from_behind(): lax.ppermute(array, axis, [(i, (i + by) % length) for i in range(length)])  29.6 us
  transfers between devices with their start and end apart: 18, of which 15 were waited for; matrix products, arithmetic and copies ran while one was open for 6% of the time, Pallas kernels for 0%

commit v1 on v0

v1 whole, which is shorter than its diff:
```python
import jax
import jax.numpy as jnp
from jax import lax
from jax.experimental import pallas as pl
from jax.experimental.pallas import tpu as pltpu
from jax.sharding import PartitionSpec as P

MESH = pl.DeviceIdType.MESH
F32 = jnp.float32
BF16 = jnp.bfloat16


def dot_nn(a, b):
    return lax.dot_general(a, b, (((1,), (0,)), ((), ())), preferred_element_type=F32)


def dot_nt(a, b):
    return lax.dot_general(a, b, (((1,), (1,)), ((), ())), preferred_element_type=F32)


def dot_tn(a, b):
    return lax.dot_general(a, b, (((0,), (0,)), ((), ())), preferred_element_type=F32)


def relay_kernel(
    state_ref, x_ref, rows_ref, comb_ref, wg_ref, wu_ref, wd_ref,
    state_out, gg_out, gu_out,
    xs, wga, wua, wda, st, sn, ppart, precv, ab, hpart, hrecv, act,
    gsend, grecv, psend, gprecv, keep,
    loc_sem, ws_send, ws_recv, wp_send, wp_recv, wf_send, wf_recv,
    pre_s, pre_r, hid_s, hid_r, act_s, act_r, st_s, st_r,
    gs_s, gs_r, gp_s, gp_r,
):
    s = lax.axis_index("section")
    e = lax.axis_index("expert")
    p = lax.axis_index("dp")
    sections = lax.axis_size("section")
    steps = st.shape[0]
    tokens = st.shape[2]
    sib = p + 1 - 2 * lax.rem(p, 2)
    pair = lax.rem(p + 2, 4)
    diag = lax.rem(sib + 2, 4)
    sib_dev = (s, e, sib)
    pair_dev = (s, e, pair)
    below = (lax.rem(s + sections - 1, sections), e, p)
    above = (lax.rem(s + 1, sections), e, p)

    def peer(k):
        return lax.rem(e + k, 4)

    def peer_dev(k):
        return (s, peer(k), p)

    def remote(src, dst, send, recv, dev):
        return pltpu.make_async_remote_copy(
            src_ref=src, dst_ref=dst, send_sem=send, recv_sem=recv,
            device_id=dev, device_id_type=MESH,
        )

    barrier = pltpu.get_barrier_semaphore()
    for dev in (peer_dev(1), peer_dev(2), peer_dev(3), sib_dev, pair_dev, below, above):
        pl.semaphore_signal(barrier, inc=1, device_id=dev, device_id_type=MESH)
    pl.semaphore_wait(barrier, 7)

    weights = ((wg_ref, wga), (wu_ref, wua), (wd_ref, wda))

    def own_to_pair(n):
        src, dst = weights[n]
        return remote(src, dst.at[p], wp_send.at[n], wp_recv.at[n], pair_dev)

    def own_to_sib(n):
        src, dst = weights[n]
        return remote(src, dst.at[p], ws_send.at[n], ws_recv.at[n], sib_dev)

    def pair_to_sib(n):
        dst = weights[n][1]
        return remote(dst.at[pair], dst.at[pair], wf_send.at[n], wf_recv.at[n], sib_dev)

    def local(n):
        src, dst = weights[n]
        return pltpu.make_async_copy(src, dst.at[p], loc_sem.at[n])

    for n in range(3):
        own_to_pair(n).start()
    for n in range(3):
        own_to_sib(n).start()
        local(n).start()

    def chosen(i):
        token = lax.broadcasted_iota(jnp.int32, (tokens, tokens), 0)
        return token == rows_ref[i]

    def sort_rows(i, carry):
        pick = jnp.where(chosen(i), 1.0, 0.0).astype(BF16)
        xs[i] = dot_nn(pick, x_ref[i]).astype(BF16)
        return carry

    lax.fori_loop(0, 2 * steps, sort_rows, 0)
    st[0] = state_ref[...]

    def pre_chunk(t, q):
        x = xs[pl.ds(2 * t, 2)].reshape(2 * tokens, xs.shape[2])
        ppart[t, q, 0] = dot_nn(x, wga[q]).astype(BF16)
        ppart[t, q, 1] = dot_nn(x, wua[q]).astype(BF16)

    def pre_copy(t, k):
        return remote(
            ppart.at[t, peer(k)], precv.at[t, k - 1], pre_s.at[t, k - 1], pre_r.at[t, k - 1], peer_dev(k)
        )

    local(0).wait()
    local(1).wait()
    pre_chunk(0, p)
    own_to_sib(0).wait_recv()
    own_to_sib(1).wait_recv()
    pre_chunk(0, sib)
    own_to_pair(0).wait_recv()
    pair_to_sib(0).start()
    own_to_pair(1).wait_recv()
    pair_to_sib(1).start()
    pre_chunk(0, pair)
    pair_to_sib(0).wait_recv()
    pair_to_sib(1).wait_recv()
    pre_chunk(0, diag)
    for k in (2, 1, 3):
        pre_copy(0, k).start()
    local(2).wait()
    own_to_pair(2).wait_recv()
    pair_to_sib(2).start()
    own_to_sib(2).wait_recv()
    pair_to_sib(2).wait_recv()

    def hid_copy(i, k):
        return remote(hpart.at[i, peer(k)], hrecv.at[i, k - 1], hid_s.at[i, k - 1], hid_r.at[i, k - 1], peer_dev(k))

    def act_copy(i, k):
        return remote(act.at[i, e], act.at[i, e], act_s.at[i, k - 1], act_r.at[i, k - 1], peer_dev(k))

    def act_arrival(i, k):
        there = lax.rem(e + 4 - k, 4)
        return remote(act.at[i, there], act.at[i, there], act_s.at[i, k - 1], act_r.at[i, k - 1], peer_dev(k))

    def st_copy(t, c):
        return remote(sn.at[t, c], st.at[t + 1, c], st_s.at[t, c], st_r.at[t, c], below if c == 0 else above)

    def step(t, carry):
        for c in range(2):
            i = 2 * t + c

            @pl.when(t > 0)
            def _():
                st_copy(t - 1, c).wait_recv()

            weight = jnp.sum(jnp.where(chosen(i), comb_ref[i], 0.0), axis=1, keepdims=True)
            slot_grads = (weight * st[t, c].astype(F32)).astype(BF16)
            for q in range(4):
                hpart[i, q] = dot_nt(slot_grads, wda[q]).astype(BF16)
            for k in (2, 1, 3):
                hid_copy(i, k).start()

        for k in (1, 2, 3):
            pre_copy(t, k).wait_recv()
        pre_gate = ppart[t, e, 0].astype(F32)
        pre_up = ppart[t, e, 1].astype(F32)
        for k in range(3):
            pre_gate += precv[t, k, 0].astype(F32)
            pre_up += precv[t, k, 1].astype(F32)
        sigma = jax.nn.sigmoid(pre_gate)
        ab[0] = pre_up * sigma * (1.0 + pre_gate * (1.0 - sigma))
        ab[1] = pre_gate * sigma

        for c in range(2):
            i = 2 * t + c
            for k in (1, 3, 2):
                hid_copy(i, k).wait_recv()
            hidden = hpart[i, e].astype(F32)
            for k in range(3):
                hidden += hrecv[i, k].astype(F32)
            act[i, e, 0] = (hidden * ab[0, c * tokens:(c + 1) * tokens]).astype(BF16)
            act[i, e, 1] = (hidden * ab[1, c * tokens:(c + 1) * tokens]).astype(BF16)
            for k in (2, 1, 3):
                act_copy(i, k).start()

        @pl.when(t < steps - 1)
        def _():
            def chunk(q, carry):
                pre_chunk(t + 1, q)
                return carry

            lax.fori_loop(0, 4, chunk, 0)
            for k in (2, 1, 3):
                pre_copy(t + 1, k).start()

        for c in range(2):
            i = 2 * t + c
            for k in (1, 3, 2):
                act_arrival(i, k).wait_recv()
            total = st[t, c].astype(F32)
            for q in range(4):
                total += dot_nt(act[i, q, 0], wga[q]) + dot_nt(act[i, q, 1], wua[q])
            sn[t, c] = total.astype(BF16)

            @pl.when(t < steps - 1)
            def _():
                st_copy(t, c).start()

        return carry

    lax.fori_loop(0, steps, step, 0)
    state_out[...] = sn[steps - 1]

    flat = xs[...].reshape(2 * steps * tokens, xs.shape[2])

    def weight_grad(q, n):
        grads = act[:, q, n].reshape(2 * steps * tokens, act.shape[4])
        return dot_tn(flat, grads)

    def sib_copy(m):
        return remote(gsend.at[m], grecv.at[m], gs_s.at[m], gs_r.at[m], sib_dev)

    def pair_copy(n):
        return remote(psend.at[n], gprecv.at[n], gp_s.at[n], gp_r.at[n], pair_dev)

    for n in range(2):
        gsend[n] = weight_grad(diag, n).astype(BF16)
        sib_copy(n).start()
        part = weight_grad(pair, n)
        sib_copy(n).wait_recv()
        psend[n] = (part + grecv[n].astype(F32)).astype(BF16)
        pair_copy(n).start()
    for n in range(2):
        gsend[2 + n] = weight_grad(sib, n).astype(BF16)
        sib_copy(2 + n).start()
    for n in range(2):
        keep[n] = weight_grad(p, n)
    for n in range(2):
        sib_copy(2 + n).wait_recv()
        keep[n] += grecv[2 + n].astype(F32)
    for n, out in ((0, gg_out), (1, gu_out)):
        pair_copy(n).wait_recv()
        out[...] = (keep[n] + gprecv[n].astype(F32)).astype(BF16)

    for n in range(3):
        own_to_pair(n).wait_send()
        own_to_sib(n).wait_send()
        pair_to_sib(n).wait_send()
    for n in range(2):
        pair_copy(n).wait_send()
    for m in range(4):
        sib_copy(m).wait_send()

    def drain(t, carry):
        for k in (1, 2, 3):
            pre_copy(t, k).wait_send()
            for c in range(2):
                hid_copy(2 * t + c, k).wait_send()
                act_copy(2 * t + c, k).wait_send()
        return carry

    lax.fori_loop(0, steps, drain, 0)
    for t in range(steps - 1):
        for c in range(2):
            st_copy(t, c).wait_send()


def on_device(state_in, saved_inputs, slot_rows, combine, w_gate, w_up, w_down):
    steps, _, _, tokens, width = saved_inputs.shape
    hidden = w_gate.shape[2]
    layers = 2 * steps
    sems = pltpu.SemaphoreType.DMA
    vmem = pl.BlockSpec(memory_space=pltpu.VMEM)
    anywhere = pl.BlockSpec(memory_space=pl.ANY)
    state_out, grad_gate, grad_up = pl.pallas_call(
        relay_kernel,
        out_shape=(
            jax.ShapeDtypeStruct((2, tokens, width), BF16),
            jax.ShapeDtypeStruct((width, hidden), BF16),
            jax.ShapeDtypeStruct((width, hidden), BF16),
        ),
        in_specs=[vmem] * 4 + [anywhere] * 3,
        out_specs=(vmem, vmem, vmem),
        scratch_shapes=[
            pltpu.VMEM((layers, tokens, width), BF16),
            pltpu.VMEM((4, width, hidden), BF16),
            pltpu.VMEM((4, width, hidden), BF16),
            pltpu.VMEM((4, hidden, width), BF16),
            pltpu.VMEM((steps, 2, tokens, width), BF16),
            pltpu.VMEM((steps, 2, tokens, width), BF16),
            pltpu.VMEM((steps, 4, 2, 2 * tokens, hidden), BF16),
            pltpu.VMEM((steps, 3, 2, 2 * tokens, hidden), BF16),
            pltpu.VMEM((2, 2 * tokens, hidden), F32),
            pltpu.VMEM((layers, 4, tokens, hidden), BF16),
            pltpu.VMEM((layers, 3, tokens, hidden), BF16),
            pltpu.VMEM((layers, 4, 2, tokens, hidden), BF16),
            pltpu.VMEM((4, width, hidden), BF16),
            pltpu.VMEM((4, width, hidden), BF16),
            pltpu.VMEM((2, width, hidden), BF16),
            pltpu.VMEM((2, width, hidden), BF16),
            pltpu.VMEM((2, width, hidden), F32),
            sems((3,)), sems((3,)), sems((3,)), sems((3,)), sems((3,)), sems((3,)), sems((3,)),
            sems((steps, 3)), sems((steps, 3)),
            sems((layers, 3)), sems((layers, 3)),
            sems((layers, 3)), sems((layers, 3)),
            sems((steps - 1, 2)), sems((steps - 1, 2)),
            sems((4,)), sems((4,)), sems((2,)), sems((2,)),
        ],
        compiler_params=pltpu.CompilerParams(
            collective_id=0, has_side_effects=True, vmem_limit_bytes=56 * 2**20
        ),
        cost_estimate=pl.CostEstimate(
            flops=2 * layers * tokens * width * 4 * hidden * 7,
            bytes_accessed=2 * (layers * tokens * width + 5 * width * hidden),
            transcendentals=layers * tokens * hidden,
        ),
        name="relay",
    )(
        state_in[:, 0],
        saved_inputs.reshape(layers, tokens, width),
        slot_rows.reshape(layers, 1, tokens),
        combine.reshape(layers, 1, tokens),
        w_gate[0],
        w_up[0],
        w_down[0],
    )
    return state_out[:, None], grad_gate[None], grad_up[None]


def solution(mesh):
    placed = (
        P(None, "section", "dp", "expert"),
        P(None, None, "section", "dp", "expert"),
        P(None, None, "section", "dp"),
        P(None, None, "section", "dp"),
        P("section", "expert", "dp"),
        P("section", "expert", "dp"),
        P("section", "dp", "expert"),
    )
    return jax.shard_map(
        on_device,
        mesh=mesh,
        in_specs=placed,
        out_specs=(
            P(None, "section", "dp", "expert"),
            P("section", "expert", "dp"),
            P("section", "expert", "dp"),
        ),
        check_vma=False,
    )
```

time: 683 us -> 212 us (0.31)
  waiting for transfers between devices: 419 us -> 0 us
  Pallas kernels: 0 us -> 207 us
  blocking collectives: 117 us -> 0 us
  matrix products: 46.2 us -> 0 us
  other arithmetic: 34.6 us -> 0 us
  starting transfers between devices: 30.3 us -> 0 us
  between operations: 15.7 us -> 0.65 us
  local copies, waits for them, and re-layouts: 11.7 us -> 3.65 us
    psum x4 -> x0, waiting for transfers between devices: 263 us -> none  [width_sums(): lax.psum(hidden_grad.astype(jnp.bfloat16), 'expert').astype(jnp.float32)]
    pallas_call x0 -> x1, Pallas kernels: none -> 207 us  [on_device(): pl.pallas_call(relay_kernel, out_shape=(jax.ShapeDtypeStruct((2, tokens,...]
    reduce_scatter x8 -> x0, waiting for transfers between devices: 151 us -> none  [section_layer(): lax.psum_scatter((first + lax.dot_general(up_grad, up_w, contract, prefer...]
    all_gather x16 -> x0, blocking collectives: 117 us -> none  [the longest x8 61.8 us: section_layer(): lax.all_gather(inputs, 'dp', axis=0, tiled=True)]
    dot_general x42 -> x0, matrix products: 46.2 us -> none  [the longest x8 11.8 us: section_layer(): lax.dot_general(up_grad, up_w, contract, preferred_element_type=jnp.float32)]
    ppermute x6 -> x0, starting transfers between devices: 29.6 us -> none  [from_behind(): lax.ppermute(array, axis, [(i, (i + by) % length) for i in range(length)])]
    scatter x8 -> x0, other arithmetic: 10.2 us -> none  [section_layer(): return (grads_state.at[slot_index].set(updated), retained)]
    another operation x11 -> x0, other arithmetic: 8.82 us -> none  [the longest x6 8.73 us: advance(): jnp.stack([retained_parts[0][place], retained_parts[1][place]])]
  transfers between devices with their start and end apart: 18 -> 0, of which waited for: 15 -> 0; matrix products, arithmetic and copies ran while one was open for 6% -> 0% of each run, Pallas kernels for 0% -> 0%
where the time goes in v1:
time: 212 us; the launch traced here: 211 us
  Pallas kernels  207 us (98%)
  local copies, waits for them, and re-layouts  3.65 us (2%)
    pallas_call x1, Pallas kernels, on_device(): pl.pallas_call(relay_kernel, out_shape=(jax.ShapeDtypeStruct((2, tokens,...  207 us

profile of v1, /device:TPU:1, one launch (start us, length us, event | category | flops | bytes accessed | tf_op | source)
XLA Modules:
  0.0 210.8 jit_solution(6992309254576083273)
XLA Ops:
  0.6 206.5 %relay.1 = (bf16[2,64,896]{2,1,0:T(8,128)(2,1)}, bf16[896,256]{1,0:T(8,128)(2,1)}, bf16[896,256]{1,0:T(8,128)(2,1)}) custom-call(bf16[2,64,896]{2,1,0:T(8,128)(2,1)} %bitcast.19, bf16[8,64,896]{2,1,0:T(8,128)(2,1)} %bitcast.15, s32[8,1,64]{2,1,0:T(1,128)} %bitcast.20, f32[8,1,64]{2,1,0:T(1,128)} %bitcast.21, bf16[896,256]{1,0:T(8,128)(2,1)} %bitcast.16, ...), custom_call_target="tpu_custom_call" | custom-call | flops 6576668672 | bytes 3211264 | tf_op jit(solution)/shard_map/relay/pallas_call | solution.py:273
  207.2 0.0 copy-start.1
  207.2 1.7 copy.14
  208.9 0.0 copy-done.1
  208.9 0.0 copy-start
  208.9 0.8 copy.15
  209.7 0.4 copy-done
  210.1 0.8 copy.16
Async XLA Ops:
  207.2 1.7 copy-start.1
  208.9 1.2 copy-start

commit v2 on v1

--- a/solution.py
+++ b/solution.py
@@ -25,11 +25,11 @@
 def relay_kernel(
     state_ref, x_ref, rows_ref, comb_ref, wg_ref, wu_ref, wd_ref,
     state_out, gg_out, gu_out,
-    xs, wga, wua, wda, st, sn, ppart, precv, ab, hpart, hrecv, act,
-    gsend, grecv, psend, gprecv, keep,
+    xs, wga, wua, wda, st, sn, ppart, via, precv, ab, hpart, hrecv, act,
+    gsend, grecv, psend, gprecv, keep, xlate, actlate,
     loc_sem, ws_send, ws_recv, wp_send, wp_recv, wf_send, wf_recv,
-    pre_s, pre_r, hid_s, hid_r, act_s, act_r, st_s, st_r,
-    gs_s, gs_r, gp_s, gp_r,
+    pre_s, pre_r, hid_s, hid_r, act_s, act_r, fwd_s, fwd_r, st_s, st_r,
+    gs_s, gs_r, gp_s, gp_r, xl_s, xl_r, al_s, al_r,
 ):
     s = lax.axis_index("section")
     e = lax.axis_index("expert")
@@ -42,6 +42,10 @@
     diag = lax.rem(sib + 2, 4)
     sib_dev = (s, e, sib)
     pair_dev = (s, e, pair)
+    diag_dev = (s, e, diag)
+    ahead, across, behind = (lax.rem(e + k, 4) for k in (1, 2, 3))
+    ahead_dev = (s, ahead, p)
+    behind_dev = (s, behind, p)
     below = (lax.rem(s + sections - 1, sections), e, p)
     above = (lax.rem(s + 1, sections), e, p)
 
@@ -58,9 +62,9 @@
         )
 
     barrier = pltpu.get_barrier_semaphore()
-    for dev in (peer_dev(1), peer_dev(2), peer_dev(3), sib_dev, pair_dev, below, above):
+    for dev in (peer_dev(1), peer_dev(2), peer_dev(3), sib_dev, pair_dev, diag_dev, below, above):
         pl.semaphore_signal(barrier, inc=1, device_id=dev, device_id_type=MESH)
-    pl.semaphore_wait(barrier, 7)
+    pl.semaphore_wait(barrier, 8)
 
     weights = ((wg_ref, wga), (wu_ref, wua), (wd_ref, wda))
 
@@ -103,10 +107,28 @@
         ppart[t, q, 0] = dot_nn(x, wga[q]).astype(BF16)
         ppart[t, q, 1] = dot_nn(x, wua[q]).astype(BF16)
 
-    def pre_copy(t, k):
-        return remote(
-            ppart.at[t, peer(k)], precv.at[t, k - 1], pre_s.at[t, k - 1], pre_r.at[t, k - 1], peer_dev(k)
-        )
+    def pre_copy(t, m):
+        src, dst, dev = (
+            (ppart.at[t, across, 0], via.at[t, 0], ahead_dev),
+            (ppart.at[t, across, 1], via.at[t, 1], behind_dev),
+            (ppart.at[t, ahead, 1], precv.at[t, 0], ahead_dev),
+            (ppart.at[t, behind, 0], precv.at[t, 1], behind_dev),
+            (ppart.at[t, ahead, 0], precv.at[t, 2], ahead_dev),
+            (ppart.at[t, behind, 1], precv.at[t, 3], behind_dev),
+        )[m]
+        return remote(src, dst, pre_s.at[t, m], pre_r.at[t, m], dev)
+
+    def pre_first(t):
+        for m in range(4):
+            pre_copy(t, m).start()
+
+    def pre_second(t):
+        pre_copy(t, 0).wait_recv()
+        ppart[t, ahead, 0] = (ppart[t, ahead, 0].astype(F32) + via[t, 0].astype(F32)).astype(BF16)
+        pre_copy(t, 4).start()
+        pre_copy(t, 1).wait_recv()
+        ppart[t, behind, 1] = (ppart[t, behind, 1].astype(F32) + via[t, 1].astype(F32)).astype(BF16)
+        pre_copy(t, 5).start()
 
     local(0).wait()
     local(1).wait()
@@ -122,8 +144,8 @@
     pair_to_sib(0).wait_recv()
     pair_to_sib(1).wait_recv()
     pre_chunk(0, diag)
-    for k in (2, 1, 3):
-        pre_copy(0, k).start()
+    pre_first(0)
+    pre_second(0)
     local(2).wait()
     own_to_pair(2).wait_recv()
     pair_to_sib(2).start()
@@ -133,12 +155,57 @@
     def hid_copy(i, k):
         return remote(hpart.at[i, peer(k)], hrecv.at[i, k - 1], hid_s.at[i, k - 1], hid_r.at[i, k - 1], peer_dev(k))
 
-    def act_copy(i, k):
-        return remote(act.at[i, e], act.at[i, e], act_s.at[i, k - 1], act_r.at[i, k - 1], peer_dev(k))
-
-    def act_arrival(i, k):
-        there = lax.rem(e + 4 - k, 4)
-        return remote(act.at[i, there], act.at[i, there], act_s.at[i, k - 1], act_r.at[i, k - 1], peer_dev(k))
+    def act_copy(i, way):
+        return remote(act.at[i, e], act.at[i, e], act_s.at[i, way], act_r.at[i, way], (ahead_dev, behind_dev)[way])
+
+    def act_arrival(i, way):
+        there = (behind, ahead)[way]
+        return remote(
+            act.at[i, there], act.at[i, there], act_s.at[i, way], act_r.at[i, way], (ahead_dev, behind_dev)[way]
+        )
+
+    def act_forward(i, way):
+        there = (behind, ahead)[way]
+        return remote(
+            act.at[i, there, way], act.at[i, there, way], fwd_s.at[i, way], fwd_r.at[i, way],
+            (ahead_dev, behind_dev)[way],
+        )
+
+    def act_last(i, way):
+        return remote(
+            act.at[i, across, way], act.at[i, across, way], fwd_s.at[i, way], fwd_r.at[i, way],
+            (ahead_dev, behind_dev)[way],
+        )
+
+    def pass_on(i):
+        for way in range(2):
+            act_arrival(i, way).wait_recv()
+            act_forward(i, way).start()
+
+    early = 2 * (steps - 1)
+
+    def weight_grad(q, n, layers):
+        rows = xs[0:layers].reshape(layers * tokens, xs.shape[2])
+        grads = act[0:layers, q, n].reshape(layers * tokens, act.shape[4])
+        return dot_tn(rows, grads)
+
+    def sib_copy(m):
+        return remote(gsend.at[m], grecv.at[m], gs_s.at[m], gs_r.at[m], sib_dev)
+
+    def pair_copy(n):
+        return remote(psend.at[n], gprecv.at[n], gp_s.at[n], gp_r.at[n], pair_dev)
+
+    def rows_copy(m):
+        src, dst, dev = (
+            (xs.at[pl.ds(early, 2)], xlate.at[p], sib_dev),
+            (xs.at[pl.ds(early, 2)], xlate.at[p], pair_dev),
+            (xlate.at[pair], xlate.at[pair], sib_dev),
+        )[m]
+        return remote(src, dst, xl_s.at[m], xl_r.at[m], dev)
+
+    def late_copy(c, m):
+        there, dev = ((sib, sib_dev), (pair, pair_dev), (diag, diag_dev))[m]
+        return remote(act.at[early + c, there], actlate.at[p, c], al_s.at[c, m], al_r.at[c, m], dev)
 
     def st_copy(t, c):
         return remote(sn.at[t, c], st.at[t + 1, c], st_s.at[t, c], st_r.at[t, c], below if c == 0 else above)
@@ -158,13 +225,10 @@
             for k in (2, 1, 3):
                 hid_copy(i, k).start()
 
-        for k in (1, 2, 3):
-            pre_copy(t, k).wait_recv()
-        pre_gate = ppart[t, e, 0].astype(F32)
-        pre_up = ppart[t, e, 1].astype(F32)
-        for k in range(3):
-            pre_gate += precv[t, k, 0].astype(F32)
-            pre_up += precv[t, k, 1].astype(F32)
+        for m in range(2, 6):
+            pre_copy(t, m).wait_recv()
+        pre_gate = ppart[t, e, 0].astype(F32) + precv[t, 1].astype(F32) + precv[t, 2].astype(F32)
+        pre_up = ppart[t, e, 1].astype(F32) + precv[t, 0].astype(F32) + precv[t, 3].astype(F32)
         sigma = jax.nn.sigmoid(pre_gate)
         ab[0] = pre_up * sigma * (1.0 + pre_gate * (1.0 - sigma))
         ab[1] = pre_gate * sigma
@@ -178,64 +242,86 @@
                 hidden += hrecv[i, k].astype(F32)
             act[i, e, 0] = (hidden * ab[0, c * tokens:(c + 1) * tokens]).astype(BF16)
             act[i, e, 1] = (hidden * ab[1, c * tokens:(c + 1) * tokens]).astype(BF16)
-            for k in (2, 1, 3):
-                act_copy(i, k).start()
+            for way in range(2):
+                act_copy(i, way).start()
 
         @pl.when(t < steps - 1)
         def _():
-            def chunk(q, carry):
+            for q in range(4):
                 pre_chunk(t + 1, q)
-                return carry
-
-            lax.fori_loop(0, 4, chunk, 0)
-            for k in (2, 1, 3):
-                pre_copy(t + 1, k).start()
+                if q == 1:
+                    pass_on(2 * t)
+            pass_on(2 * t + 1)
+            pre_first(t + 1)
+
+        @pl.when(t == steps - 1)
+        def _():
+            rows_copy(1).start()
+            rows_copy(0).start()
+            for n in range(2):
+                gsend[n] = weight_grad(diag, n, early).astype(BF16)
+                sib_copy(n).start()
+            pass_on(2 * t)
+            for n in range(2):
+                keep[n] = weight_grad(pair, n, early)
+            pass_on(2 * t + 1)
+            for n in range(2):
+                sib_copy(n).wait_recv()
+                psend[n] = (keep[n] + grecv[n].astype(F32)).astype(BF16)
+                pair_copy(n).start()
 
         for c in range(2):
             i = 2 * t + c
-            for k in (1, 3, 2):
-                act_arrival(i, k).wait_recv()
             total = st[t, c].astype(F32)
-            for q in range(4):
+            for q in (e, behind, ahead):
                 total += dot_nt(act[i, q, 0], wga[q]) + dot_nt(act[i, q, 1], wua[q])
+            for way in range(2):
+                act_last(i, way).wait_recv()
+
+            @pl.when(t == steps - 1)
+            def _():
+                for m in (2, 1, 0):
+                    late_copy(c, m).start()
+
+            total += dot_nt(act[i, across, 0], wga[across]) + dot_nt(act[i, across, 1], wua[across])
             sn[t, c] = total.astype(BF16)
 
             @pl.when(t < steps - 1)
             def _():
                 st_copy(t, c).start()
 
+        @pl.when(t < steps - 1)
+        def _():
+            pre_second(t + 1)
+
         return carry
 
     lax.fori_loop(0, steps, step, 0)
     state_out[...] = sn[steps - 1]
 
-    flat = xs[...].reshape(2 * steps * tokens, xs.shape[2])
-
-    def weight_grad(q, n):
-        grads = act[:, q, n].reshape(2 * steps * tokens, act.shape[4])
-        return dot_tn(flat, grads)
-
-    def sib_copy(m):
-        return remote(gsend.at[m], grecv.at[m], gs_s.at[m], gs_r.at[m], sib_dev)
-
-    def pair_copy(n):
-        return remote(psend.at[n], gprecv.at[n], gp_s.at[n], gp_r.at[n], pair_dev)
-
     for n in range(2):
-        gsend[n] = weight_grad(diag, n).astype(BF16)
-        sib_copy(n).start()
-        part = weight_grad(pair, n)
-        sib_copy(n).wait_recv()
-        psend[n] = (part + grecv[n].astype(F32)).astype(BF16)
-        pair_copy(n).start()
+        gsend[2 + n] = weight_grad(sib, n, early).astype(BF16)
+        sib_copy(2 + n).start()
+    rows_copy(1).wait_recv()
+    rows_copy(2).start()
     for n in range(2):
-        gsend[2 + n] = weight_grad(sib, n).astype(BF16)
-        sib_copy(2 + n).start()
-    for n in range(2):
-        keep[n] = weight_grad(p, n)
+        keep[n] = weight_grad(p, n, 2 * steps)
+
+    def add_late(there, m):
+        for c in range(2):
+            late_copy(c, m).wait_recv()
+        rows = xlate[there].reshape(2 * tokens, xs.shape[2])
+        for n in range(2):
+            keep[n] += dot_tn(rows, actlate[there, :, n].reshape(2 * tokens, act.shape[4]))
+
+    rows_copy(0).wait_recv()
+    add_late(sib, 0)
     for n in range(2):
         sib_copy(2 + n).wait_recv()
         keep[n] += grecv[2 + n].astype(F32)
+    add_late(pair, 1)
+    rows_copy(2).wait_recv()
+    add_late(diag, 2)
     for n, out in ((0, gg_out), (1, gu_out)):
         pair_copy(n).wait_recv()
         out[...] = (keep[n] + gprecv[n].astype(F32)).astype(BF16)
@@ -248,13 +334,20 @@
         pair_copy(n).wait_send()
     for m in range(4):
         sib_copy(m).wait_send()
+    for m in range(3):
+        rows_copy(m).wait_send()
+        for c in range(2):
+            late_copy(c, m).wait_send()
 
     def drain(t, carry):
-        for k in (1, 2, 3):
-            pre_copy(t, k).wait_send()
-            for c in range(2):
+        for m in range(6):
+            pre_copy(t, m).wait_send()
+        for c in range(2):
+            for k in (1, 2, 3):
                 hid_copy(2 * t + c, k).wait_send()
-                act_copy(2 * t + c, k).wait_send()
+            for way in range(2):
+                act_copy(2 * t + c, way).wait_send()
+                act_forward(2 * t + c, way).wait_send()
         return carry
 
     lax.fori_loop(0, steps, drain, 0)
@@ -287,7 +380,8 @@
             pltpu.VMEM((steps, 2, tokens, width), BF16),
             pltpu.VMEM((steps, 2, tokens, width), BF16),
             pltpu.VMEM((steps, 4, 2, 2 * tokens, hidden), BF16),
-            pltpu.VMEM((steps, 3, 2, 2 * tokens, hidden), BF16),
+            pltpu.VMEM((steps, 2, 2 * tokens, hidden), BF16),
+            pltpu.VMEM((steps, 4, 2 * tokens, hidden), BF16),
             pltpu.VMEM((2, 2 * tokens, hidden), F32),
             pltpu.VMEM((layers, 4, tokens, hidden), BF16),
             pltpu.VMEM((layers, 3, tokens, hidden), BF16),
@@ -297,12 +391,16 @@
             pltpu.VMEM((2, width, hidden), BF16),
             pltpu.VMEM((2, width, hidden), BF16),
             pltpu.VMEM((2, width, hidden), F32),
+            pltpu.VMEM((4, 2, tokens, width), BF16),
+            pltpu.VMEM((4, 2, 2, tokens, hidden), BF16),
             sems((3,)), sems((3,)), sems((3,)), sems((3,)), sems((3,)), sems((3,)), sems((3,)),
-            sems((steps, 3)), sems((steps, 3)),
+            sems((steps, 6)), sems((steps, 6)),
             sems((layers, 3)), sems((layers, 3)),
-            sems((layers, 3)), sems((layers, 3)),
+            sems((layers, 2)), sems((layers, 2)),
+            sems((layers, 2)), sems((layers, 2)),
             sems((steps - 1, 2)), sems((steps - 1, 2)),
             sems((4,)), sems((4,)), sems((2,)), sems((2,)),
+            sems((3,)), sems((3,)), sems((2, 3)), sems((2, 3)),
         ],
         compiler_params=pltpu.CompilerParams(
             collective_id=0, has_side_effects=True, vmem_limit_bytes=56 * 2**20

time: 212 us -> 184 us (0.87)
  Pallas kernels: 207 us -> 179 us
    pallas_call x1, Pallas kernels: 207 us -> 179 us  [on_device(): pl.pallas_call(relay_kernel, out_shape=(jax.ShapeDtypeStruct((2, tokens,...]
where the time goes in v2:
time: 184 us
  Pallas kernels  179 us (97%)
  local copies, waits for them, and re-layouts  3.65 us (2%)
    pallas_call x1, Pallas kernels, on_device(): pl.pallas_call(relay_kernel, out_shape=(jax.ShapeDtypeStruct((2, tokens,...  179 us

profile of v2, /device:TPU:1, one launch (start us, length us, event | category | flops | bytes accessed | tf_op | source)
XLA Modules:
  0.0 183.6 jit_solution(2958199552461310296)
XLA Ops:
  0.6 179.3 %relay.1 = (bf16[2,64,896]{2,1,0:T(8,128)(2,1)}, bf16[896,256]{1,0:T(8,128)(2,1)}, bf16[896,256]{1,0:T(8,128)(2,1)}) custom-call(bf16[2,64,896]{2,1,0:T(8,128)(2,1)} %bitcast.19, bf16[8,64,896]{2,1,0:T(8,128)(2,1)} %bitcast.15, s32[8,1,64]{2,1,0:T(1,128)} %bitcast.20, f32[8,1,64]{2,1,0:T(1,128)} %bitcast.21, bf16[896,256]{1,0:T(8,128)(2,1)} %bitcast.16, ...), custom_call_target="tpu_custom_call" | custom-call | flops 6576668672 | bytes 3211264 | tf_op jit(solution)/shard_map/relay/pallas_call | solution.py:366
  179.9 0.0 copy-start.1
  180.0 1.7 copy.14
  181.7 0.0 copy-done.1
  181.7 0.0 copy-start
  181.7 0.8 copy.15
  182.4 0.4 copy-done
  182.8 0.8 copy.16
Async XLA Ops:
  179.9 1.7 copy-start.1
  181.7 1.2 copy-start

commit v3 on v1

v3 whole, which is shorter than its diff:
```python
import jax
import jax.numpy as jnp
from jax import lax
from jax.experimental import pallas as pl
from jax.experimental.pallas import tpu as pltpu
from jax.sharding import PartitionSpec as P

MESH = pl.DeviceIdType.MESH
F32 = jnp.float32
BF16 = jnp.bfloat16


def dot_nn(a, b):
    return lax.dot_general(a, b, (((1,), (0,)), ((), ())), preferred_element_type=F32)


def dot_nt(a, b):
    return lax.dot_general(a, b, (((1,), (1,)), ((), ())), preferred_element_type=F32)


def dot_tn(a, b):
    return lax.dot_general(a, b, (((0,), (0,)), ((), ())), preferred_element_type=F32)


def relay_kernel(
    state_ref, x_ref, rows_ref, comb_ref, wg_ref, wu_ref, wd_ref,
    state_out, gg_out, gu_out,
    xraw, xhome, rows, comb, xs, wga, wua, wda, st, sn, back, ppart, via, precv, ab, hpart, hvia, hrecv, act,
    actlate, keep,
    loc_sem, home_sem, ws_send, ws_recv, wp_send, wp_recv, wf_send, wf_recv, in_s, in_r,
    pre_s, pre_r, hid_s, hid_r, act_s, act_r, st_s, st_r, back_s, back_r, xl_s, xl_r, al_s, al_r,
):
    s = lax.axis_index("section")
    e = lax.axis_index("expert")
    p = lax.axis_index("dp")
    sections = lax.axis_size("section")
    steps = st.shape[0]
    tokens = st.shape[2]
    core = lax.rem(p, 2)
    low = lax.div(p, 2)
    sib = p + 1 - 2 * core
    pair = lax.rem(p + 2, 4)
    diag = lax.rem(sib + 2, 4)
    sib_dev = (s, e, sib)
    pair_dev = (s, e, pair)
    diag_dev = (s, e, diag)
    below = (lax.rem(s + sections - 1, sections), e, p)
    above = (lax.rem(s + 1, sections), e, p)

    swapped = lax.rem(e + core, 2) == 1
    near = lax.rem(e + 3 + 2 * low, 4)
    far = lax.rem(e + 1 + 2 * low, 4)
    oppo = lax.rem(e + 2, 4)
    near_dev = (s, near, pair)
    far_dev = (s, far, pair)
    oppo_dev = (s, oppo, p)

    def remote(src, dst, send, recv, dev):
        return pltpu.make_async_remote_copy(
            src_ref=src, dst_ref=dst, send_sem=send, recv_sem=recv,
            device_id=dev, device_id_type=MESH,
        )

    barrier = pltpu.get_barrier_semaphore()
    for dev in (near_dev, far_dev, oppo_dev, sib_dev, pair_dev, diag_dev, below, above):
        pl.semaphore_signal(barrier, inc=1, device_id=dev, device_id_type=MESH)
    pl.semaphore_wait(barrier, 8)

    def input_refs(m):
        if m == 0:
            return state_ref, st.at[0]
        if m == 1:
            return rows_ref, rows
        if m == 2:
            return comb_ref, comb
        return x_ref.at[pl.ds(2 * (m - 3), 2)], xraw.at[pl.ds(2 * (m - 3), 2)]

    def swap_copy(m):
        src, dst = input_refs(m)
        return remote(src, dst, in_s.at[m], in_r.at[m], pair_dev)

    def stay_copy(m):
        src, dst = input_refs(m)
        return pltpu.make_async_copy(src, dst, in_r.at[m])

    def input_start(members):
        @pl.when(swapped)
        def _():
            for m in members:
                swap_copy(m).start()

        @pl.when(jnp.logical_not(swapped))
        def _():
            for m in members:
                stay_copy(m).start()

    def input_wait(members):
        @pl.when(swapped)
        def _():
            for m in members:
                swap_copy(m).wait_recv()

        @pl.when(jnp.logical_not(swapped))
        def _():
            for m in members:
                stay_copy(m).wait()

    def weight_refs(n):
        src, dst = ((wg_ref, wga), (wu_ref, wua), (wd_ref, wda))[n // 2]
        depth = src.shape[0] // 2
        return src, dst, pl.ds((n % 2) * depth, depth)

    def own_to_pair(n):
        src, dst, part = weight_refs(n)
        return remote(src.at[part], dst.at[p, part], wp_send.at[n], wp_recv.at[n], pair_dev)

    def own_to_sib(n):
        src, dst, part = weight_refs(n)
        return remote(src.at[part], dst.at[p, part], ws_send.at[n], ws_recv.at[n], sib_dev)

    def pair_to_sib(n):
        src, dst, part = weight_refs(n)
        return remote(dst.at[pair, part], dst.at[pair, part], wf_send.at[n], wf_recv.at[n], sib_dev)

    def local(n):
        src, dst, part = weight_refs(n)
        return pltpu.make_async_copy(src.at[part], dst.at[p, part], loc_sem.at[n])

    def forward(n):
        own_to_pair(n).wait_recv()
        pair_to_sib(n).start()
        if n + 3 < 6:
            own_to_pair(n + 3).start()

    home = pltpu.make_async_copy(x_ref, xhome, home_sem.at[0])

    input_start((1, 2, 3))
    for n in range(3):
        own_to_pair(n).start()
    for n in range(6):
        local(n).start()
        own_to_sib(n).start()
    home.start()

    def chosen(of, i):
        token = lax.broadcasted_iota(jnp.int32, (tokens, tokens), 0)
        return token == of[i]

    def sort_rows(t, of, raw, there):
        for c in range(2):
            i = 2 * t + c
            pick = jnp.where(chosen(of, i), 1.0, 0.0).astype(BF16)
            xs[there, i] = dot_nn(pick, raw[i]).astype(BF16)

    def pre_chunk(t, q):
        x = xs[p, pl.ds(2 * t, 2)].reshape(2 * tokens, xs.shape[3])
        ppart[t, q, 0] = dot_nn(x, wga[q]).astype(BF16)
        ppart[t, q, 1] = dot_nn(x, wua[q]).astype(BF16)

    def pre_copy(t, m):
        src, dst, dev = (
            (ppart.at[t, near], via.at[t, 0], near_dev),
            (ppart.at[t, oppo], via.at[t, 1], near_dev),
            (ppart.at[t, far], precv.at[t], far_dev),
        )[m]
        return remote(src, dst, pre_s.at[t, m], pre_r.at[t, m], dev)

    def pre_second(t):
        pre_copy(t, 1).wait_recv()
        for n in range(2):
            ppart[t, far, n] = (ppart[t, far, n].astype(F32) + via[t, 1, n].astype(F32)).astype(BF16)
        pre_copy(t, 2).start()

    def rows_copy(t, m):
        there, dev = ((p, sib_dev), (p, pair_dev), (pair, sib_dev))[m]
        part = pl.ds(2 * t, 2)
        return remote(xs.at[there, part], xs.at[there, part], xl_s.at[t, m], xl_r.at[t, m], dev)

    def rows_first(t):
        rows_copy(t, 0).start()

        @pl.when(jnp.logical_not(swapped))
        def _():
            rows_copy(t, 1).start()

    def rows_second(t):
        @pl.when(swapped)
        def _():
            sort_rows(t, rows_ref, xhome, pair)

        @pl.when(jnp.logical_not(swapped))
        def _():
            there, part = pair, pl.ds(2 * t, 2)
            remote(
                xs.at[there, part], xs.at[there, part], xl_s.at[t, 1], xl_r.at[t, 1], pair_dev
            ).wait_recv()

        rows_copy(t, 2).start()

    input_wait((1, 2, 3))
    sort_rows(0, rows, xraw, p)
    for n in range(4):
        local(n).wait()
    pre_chunk(0, p)
    forward(0)
    for n in range(4):
        own_to_sib(n).wait_recv()
    pre_chunk(0, sib)
    for n in range(1, 4):
        forward(n)
    input_start((0,))
    pre_chunk(0, pair)
    for n in range(4):
        pair_to_sib(n).wait_recv()
    pre_chunk(0, diag)
    pre_copy(0, 1).start()
    pre_copy(0, 0).start()
    home.wait()
    forward(4)
    for n in (4, 5):
        local(n).wait()
        own_to_sib(n).wait_recv()
    forward(5)
    pre_second(0)
    input_start((4,))
    rows_first(0)
    input_wait((0,))

    def hid_copy(i, m):
        src, dst, dev = (
            (hpart.at[i, near], hvia.at[i, 0], near_dev),
            (hpart.at[i, oppo], hvia.at[i, 1], near_dev),
            (hpart.at[i, far], hrecv.at[i], far_dev),
        )[m]
        return remote(src, dst, hid_s.at[i, m], hid_r.at[i, m], dev)

    def act_copy(i, m):
        q, dev = ((e, near_dev), (e, far_dev), (far, near_dev))[m]
        return remote(act.at[i, q], act.at[i, q], act_s.at[i, m], act_r.at[i, m], dev)

    def act_arrival(i, m):
        q, dev = ((near, near_dev), (far, far_dev), (oppo, near_dev))[m]
        return remote(act.at[i, q], act.at[i, q], act_s.at[i, m], act_r.at[i, m], dev)

    def pass_on(i):
        act_arrival(i, 1).wait_recv()
        act_copy(i, 2).start()

    def late_copy(i, m):
        there, dev = ((sib, sib_dev), (pair, pair_dev), (diag, diag_dev))[m]
        return remote(act.at[i, there], actlate.at[p, i], al_s.at[i, m], al_r.at[i, m], dev)

    def weight_grad(there, grads, first, layers):
        flat = xs[there, first:first + layers].reshape(layers * tokens, xs.shape[3])
        return [
            dot_tn(flat, grads[first:first + layers, n].reshape(layers * tokens, act.shape[4])) for n in range(2)
        ]

    def add_others(there, m, first, layers):
        for i in range(first, first + layers):
            late_copy(i, m).wait_recv()
        for n, grad in enumerate(weight_grad(there, actlate.at[there], first, layers)):
            keep[n] += grad

    def rows_arrive(t, m):
        there, part = ((sib, diag)[m // 2], pl.ds(2 * t, 2))
        remote(xs.at[there, part], xs.at[there, part], xl_s.at[t, m], xl_r.at[t, m], sib_dev).wait_recv()

    early = 2 * (steps - 1)

    def st_copy(t, c):
        return remote(sn.at[t, c], st.at[t + 1, c], st_s.at[t, c], st_r.at[t, c], below if c == 0 else above)

    def back_copy(c):
        return remote(sn.at[steps - 1, c], back.at[c], back_s.at[c], back_r.at[c], pair_dev)

    def step(t, carry):
        for c in range(2):
            i = 2 * t + c

            @pl.when(t > 0)
            def _():
                st_copy(t - 1, c).wait_recv()

            weight = jnp.sum(jnp.where(chosen(rows, i), comb[i], 0.0), axis=1, keepdims=True)
            slot_grads = (weight * st[t, c].astype(F32)).astype(BF16)
            if c == 0:
                @pl.when(t == 0)
                def _():
                    for n in (4, 5):
                        pair_to_sib(n).wait_recv()

            for m, q in ((1, oppo), (0, near)):
                hpart[i, q] = dot_nt(slot_grads, wda[q]).astype(BF16)
                hid_copy(i, m).start()
            for q in (far, e):
                hpart[i, q] = dot_nt(slot_grads, wda[q]).astype(BF16)

        for c in range(2):
            i = 2 * t + c
            hid_copy(i, 1).wait_recv()
            hpart[i, far] = (hpart[i, far].astype(F32) + hvia[i, 1].astype(F32)).astype(BF16)
            hid_copy(i, 2).start()

        for ahead in range(2, steps):
            @pl.when(t == ahead - 2)
            def _():
                input_start((3 + ahead,))

        pre_copy(t, 0).wait_recv()
        pre_copy(t, 2).wait_recv()
        pre_gate, pre_up = (
            ppart[t, e, n].astype(F32) + via[t, 0, n].astype(F32) + precv[t, n].astype(F32) for n in range(2)
        )
        sigma = jax.nn.sigmoid(pre_gate)
        ab[0] = pre_up * sigma * (1.0 + pre_gate * (1.0 - sigma))
        ab[1] = pre_gate * sigma

        for c in range(2):
            i = 2 * t + c
            for m in (0, 2):
                hid_copy(i, m).wait_recv()
            hidden = hpart[i, e].astype(F32) + hvia[i, 0].astype(F32) + hrecv[i].astype(F32)
            act[i, e, 0] = (hidden * ab[0, c * tokens:(c + 1) * tokens]).astype(BF16)
            act[i, e, 1] = (hidden * ab[1, c * tokens:(c + 1) * tokens]).astype(BF16)
            act_copy(i, 1).start()
            act_copy(i, 0).start()

        rows_second(t)
        for ahead in range(1, steps):
            @pl.when(t == ahead - 1)
            def _():
                input_wait((3 + ahead,))

        @pl.when(t < steps - 1)
        def _():
            sort_rows(t + 1, rows, xraw, p)
            pre_chunk(t + 1, oppo)
            pre_chunk(t + 1, near)
            pass_on(2 * t)
            pre_chunk(t + 1, far)
            pass_on(2 * t + 1)
            pre_copy(t + 1, 1).start()
            pre_copy(t + 1, 0).start()
            pre_chunk(t + 1, e)

        @pl.when(t == steps - 1)
        def _():
            for n, grad in enumerate(weight_grad(p, act.at[:, p], 0, early)):
                keep[n] = grad
            pass_on(2 * t)
            for ahead in range(steps - 1):
                rows_arrive(ahead, 0)
            add_others(sib, 0, 0, early)
            pass_on(2 * t + 1)
            add_others(pair, 1, 0, early)
            for ahead in range(steps - 1):
                rows_arrive(ahead, 2)
            add_others(diag, 2, 0, early)

        for c in range(2):
            i = 2 * t + c
            total = st[t, c].astype(F32)
            for q in (e, far, near):
                if q is near:
                    act_arrival(i, 0).wait_recv()
                total += dot_nt(act[i, q, 0], wga[q]) + dot_nt(act[i, q, 1], wua[q])
            act_arrival(i, 2).wait_recv()

            total += dot_nt(act[i, oppo, 0], wga[oppo]) + dot_nt(act[i, oppo, 1], wua[oppo])
            sn[t, c] = total.astype(BF16)

            @pl.when(t < steps - 1)
            def _():
                st_copy(t, c).start()

            for m in (2, 1, 0):
                late_copy(i, m).start()

        @pl.when(t < steps - 1)
        def _():
            pre_second(t + 1)
            rows_first(t + 1)

        return carry

    lax.fori_loop(0, steps, step, 0)

    @pl.when(swapped)
    def _():
        for c in range(2):
            back_copy(c).start()

    for n, grad in enumerate(weight_grad(p, act.at[:, p], early, 2)):
        keep[n] += grad
    rows_arrive(steps - 1, 0)
    add_others(sib, 0, early, 2)
    rows_arrive(steps - 1, 2)
    add_others(diag, 2, early, 2)
    add_others(pair, 1, early, 2)
    for n, out in ((0, gg_out), (1, gu_out)):
        out[...] = keep[n].astype(BF16)

    @pl.when(swapped)
    def _():
        for c in range(2):
            back_copy(c).wait_recv()
            state_out[c] = back[c]

    @pl.when(jnp.logical_not(swapped))
    def _():
        state_out[...] = sn[steps - 1]

    @pl.when(swapped)
    def _():
        for m in range(3 + steps):
            swap_copy(m).wait_send()
        for c in range(2):
            back_copy(c).wait_send()

    for n in range(6):
        own_to_pair(n).wait_send()
        own_to_sib(n).wait_send()
        pair_to_sib(n).wait_send()
    def drain(t, carry):
        for m in range(3):
            pre_copy(t, m).wait_send()
            for c in range(2):
                hid_copy(2 * t + c, m).wait_send()
                act_copy(2 * t + c, m).wait_send()
                late_copy(2 * t + c, m).wait_send()
        rows_copy(t, 0).wait_send()
        rows_copy(t, 2).wait_send()

        @pl.when(jnp.logical_not(swapped))
        def _():
            rows_copy(t, 1).wait_send()

        return carry

    lax.fori_loop(0, steps, drain, 0)
    for t in range(steps - 1):
        for c in range(2):
            st_copy(t, c).wait_send()


def on_device(state_in, saved_inputs, slot_rows, combine, w_gate, w_up, w_down):
    steps, _, _, tokens, width = saved_inputs.shape
    hidden = w_gate.shape[2]
    layers = 2 * steps
    sems = pltpu.SemaphoreType.DMA
    vmem = pl.BlockSpec(memory_space=pltpu.VMEM)
    anywhere = pl.BlockSpec(memory_space=pl.ANY)
    state_out, grad_gate, grad_up = pl.pallas_call(
        relay_kernel,
        out_shape=(
            jax.ShapeDtypeStruct((2, tokens, width), BF16),
            jax.ShapeDtypeStruct((width, hidden), BF16),
            jax.ShapeDtypeStruct((width, hidden), BF16),
        ),
        in_specs=[anywhere, anywhere, vmem, vmem] + [anywhere] * 3,
        out_specs=(vmem, vmem, vmem),
        scratch_shapes=[
            pltpu.VMEM((layers, tokens, width), BF16),
            pltpu.VMEM((layers, tokens, width), BF16),
            pltpu.VMEM((layers, 1, tokens), jnp.int32),
            pltpu.VMEM((layers, 1, tokens), F32),
            pltpu.VMEM((4, layers, tokens, width), BF16),
            pltpu.VMEM((4, width, hidden), BF16),
            pltpu.VMEM((4, width, hidden), BF16),
            pltpu.VMEM((4, hidden, width), BF16),
            pltpu.VMEM((steps, 2, tokens, width), BF16),
            pltpu.VMEM((steps, 2, tokens, width), BF16),
            pltpu.VMEM((2, tokens, width), BF16),
            pltpu.VMEM((steps, 4, 2, 2 * tokens, hidden), BF16),
            pltpu.VMEM((steps, 2, 2, 2 * tokens, hidden), BF16),
            pltpu.VMEM((steps, 2, 2 * tokens, hidden), BF16),
            pltpu.VMEM((2, 2 * tokens, hidden), F32),
            pltpu.VMEM((layers, 4, tokens, hidden), BF16),
            pltpu.VMEM((layers, 2, tokens, hidden), BF16),
            pltpu.VMEM((layers, tokens, hidden), BF16),
            pltpu.VMEM((layers, 4, 2, tokens, hidden), BF16),
            pltpu.VMEM((4, layers, 2, tokens, hidden), BF16),
            pltpu.VMEM((2, width, hidden), F32),
            sems((6,)), sems((1,)), sems((6,)), sems((6,)), sems((6,)), sems((6,)), sems((6,)), sems((6,)),
            sems((3 + steps,)), sems((3 + steps,)),
            sems((steps, 3)), sems((steps, 3)),
            sems((layers, 3)), sems((layers, 3)),
            sems((layers, 3)), sems((layers, 3)),
            sems((steps - 1, 2)), sems((steps - 1, 2)),
            sems((2,)), sems((2,)),
            sems((steps, 3)), sems((steps, 3)),
            sems((layers, 3)), sems((layers, 3)),
        ],
        compiler_params=pltpu.CompilerParams(
            collective_id=0, has_side_effects=True, vmem_limit_bytes=56 * 2**20
        ),
        cost_estimate=pl.CostEstimate(
            flops=2 * layers * tokens * width * 4 * hidden * 7,
            bytes_accessed=2 * (layers * tokens * width + 5 * width * hidden),
            transcendentals=layers * tokens * hidden,
        ),
        name="relay",
    )(
        state_in[:, 0],
        saved_inputs.reshape(layers, tokens, width),
        slot_rows.reshape(layers, 1, tokens),
        combine.reshape(layers, 1, tokens),
        w_gate[0],
        w_up[0],
        w_down[0],
    )
    return state_out[:, None], grad_gate[None], grad_up[None]


def solution(mesh):
    placed = (
        P(None, "section", "dp", "expert"),
        P(None, None, "section", "dp", "expert"),
        P(None, None, "section", "dp"),
        P(None, None, "section", "dp"),
        P("section", "expert", "dp"),
        P("section", "expert", "dp"),
        P("section", "dp", "expert"),
    )
    return jax.shard_map(
        on_device,
        mesh=mesh,
        in_specs=placed,
        out_specs=(
            P(None, "section", "dp", "expert"),
            P("section", "expert", "dp"),
            P("section", "expert", "dp"),
        ),
        check_vma=False,
    )
```

time: 212 us -> 178 us (0.84)
  Pallas kernels: 207 us -> 174 us
    pallas_call x1, Pallas kernels: 207 us -> 174 us  [on_device(): pl.pallas_call(relay_kernel, out_shape=(jax.ShapeDtypeStruct((2, tokens,...]
where the time goes in v3:
time: 178 us
  Pallas kernels  174 us (98%)
  local copies, waits for them, and re-layouts  3.65 us (2%)
    pallas_call x1, Pallas kernels, on_device(): pl.pallas_call(relay_kernel, out_shape=(jax.ShapeDtypeStruct((2, tokens,...  174 us
    unnamed x7, local copies, waits for them, and re-layouts  3.65 us

profile of v3, /device:TPU:1, one launch (start us, length us, event | category | flops | bytes accessed | tf_op | source)
XLA Modules:
  0.0 178.1 jit_solution(12432885757724838332)
XLA Ops:
  0.6 173.7 %relay.1 = (bf16[2,64,896]{2,1,0:T(8,128)(2,1)}, bf16[896,256]{1,0:T(8,128)(2,1)}, bf16[896,256]{1,0:T(8,128)(2,1)}) custom-call(bf16[2,64,896]{2,1,0:T(8,128)(2,1)} %bitcast.19, bf16[8,64,896]{2,1,0:T(8,128)(2,1)} %bitcast.15, s32[8,1,64]{2,1,0:T(1,128)} %bitcast.20, f32[8,1,64]{2,1,0:T(1,128)} %bitcast.21, bf16[896,256]{1,0:T(8,128)(2,1)} %bitcast.16, ...), custom_call_target="tpu_custom_call" | custom-call | flops 6576668672 | bytes 3211264 | tf_op jit(solution)/shard_map/relay/pallas_call | solution.py:454
  174.4 0.0 copy-start.1
  174.4 1.7 copy.14
  176.1 0.0 copy-done.1
  176.1 0.0 copy-start
  176.1 0.8 copy.15
  176.9 0.4 copy-done
  177.3 0.8 copy.16
Async XLA Ops:
  174.4 1.7 copy-start.1
  176.1 1.2 copy-start

commit v4 on v3

--- a/solution.py
+++ b/solution.py
@@ -302,11 +302,6 @@
             hpart[i, far] = (hpart[i, far].astype(F32) + hvia[i, 1].astype(F32)).astype(BF16)
             hid_copy(i, 2).start()
 
-        for ahead in range(2, steps):
-            @pl.when(t == ahead - 2)
-            def _():
-                input_start((3 + ahead,))
-
         pre_copy(t, 0).wait_recv()
         pre_copy(t, 2).wait_recv()
         pre_gate, pre_up = (
@@ -342,7 +337,13 @@
             pass_on(2 * t + 1)
             pre_copy(t + 1, 1).start()
             pre_copy(t + 1, 0).start()
+            rows_first(t + 1)
             pre_chunk(t + 1, e)
+
+        for ahead in range(2, steps):
+            @pl.when(t == ahead - 2)
+            def _():
+                input_start((3 + ahead,))
 
         @pl.when(t == steps - 1)
         def _():
@@ -380,7 +381,6 @@
         @pl.when(t < steps - 1)
         def _():
             pre_second(t + 1)
-            rows_first(t + 1)
 
         return carry
 

time: 178 us -> 176 us (0.989)
  Pallas kernels: 174 us -> 172 us
    pallas_call x1, Pallas kernels: 174 us -> 172 us  [on_device(): pl.pallas_call(relay_kernel, out_shape=(jax.ShapeDtypeStruct((2, tokens,...]
where the time goes in v4:
time: 176 us
  Pallas kernels  172 us (98%)
  local copies, waits for them, and re-layouts  3.65 us (2%)
    pallas_call x1, Pallas kernels, on_device(): pl.pallas_call(relay_kernel, out_shape=(jax.ShapeDtypeStruct((2, tokens,...  172 us
    unnamed x7, local copies, waits for them, and re-layouts  3.65 us

profile of v4, /device:TPU:1, one launch (start us, length us, event | category | flops | bytes accessed | tf_op | source)
XLA Modules:
  0.0 176.0 jit_solution(572300508659531294)
XLA Ops:
  0.6 171.7 %relay.1 = (bf16[2,64,896]{2,1,0:T(8,128)(2,1)}, bf16[896,256]{1,0:T(8,128)(2,1)}, bf16[896,256]{1,0:T(8,128)(2,1)}) custom-call(bf16[2,64,896]{2,1,0:T(8,128)(2,1)} %bitcast.19, bf16[8,64,896]{2,1,0:T(8,128)(2,1)} %bitcast.15, s32[8,1,64]{2,1,0:T(1,128)} %bitcast.20, f32[8,1,64]{2,1,0:T(1,128)} %bitcast.21, bf16[896,256]{1,0:T(8,128)(2,1)} %bitcast.16, ...), custom_call_target="tpu_custom_call" | custom-call | flops 6576668672 | bytes 3211264 | tf_op jit(solution)/shard_map/relay/pallas_call | solution.py:454
  172.4 0.0 copy-start.1
  172.4 1.7 copy.14
  174.1 0.0 copy-done.1
  174.1 0.0 copy-start
  174.1 0.8 copy.15
  174.9 0.4 copy-done
  175.3 0.8 copy.16
Async XLA Ops:
  172.4 1.7 copy-start.1
  174.1 1.2 copy-start

commit v5 on v4

--- a/solution.py
+++ b/solution.py
@@ -375,12 +375,16 @@
             def _():
                 st_copy(t, c).start()
 
-            for m in (2, 1, 0):
-                late_copy(i, m).start()
+            if c == 0:
+                for m in (2, 1, 0):
+                    late_copy(i, m).start()
 
         @pl.when(t < steps - 1)
         def _():
             pre_second(t + 1)
+
+        for m in (2, 1, 0):
+            late_copy(2 * t + 1, m).start()
 
         return carry
 

time: 176 us -> 175 us (level)
  Pallas kernels: 172 us -> 170 us
where the time goes in v5:
time: 175 us
  Pallas kernels  170 us (97%)
  local copies, waits for them, and re-layouts  3.65 us (2%)
    pallas_call x1, Pallas kernels, on_device(): pl.pallas_call(relay_kernel, out_shape=(jax.ShapeDtypeStruct((2, tokens,...  170 us
    unnamed x7, local copies, waits for them, and re-layouts  3.65 us

profile of v5, /device:TPU:1, one launch (start us, length us, event | category | flops | bytes accessed | tf_op | source)
XLA Modules:
  0.0 174.6 jit_solution(12198712348692197151)
XLA Ops:
  0.6 170.3 %relay.1 = (bf16[2,64,896]{2,1,0:T(8,128)(2,1)}, bf16[896,256]{1,0:T(8,128)(2,1)}, bf16[896,256]{1,0:T(8,128)(2,1)}) custom-call(bf16[2,64,896]{2,1,0:T(8,128)(2,1)} %bitcast.19, bf16[8,64,896]{2,1,0:T(8,128)(2,1)} %bitcast.15, s32[8,1,64]{2,1,0:T(1,128)} %bitcast.20, f32[8,1,64]{2,1,0:T(1,128)} %bitcast.21, bf16[896,256]{1,0:T(8,128)(2,1)} %bitcast.16, ...), custom_call_target="tpu_custom_call" | custom-call | flops 6576668672 | bytes 3211264 | tf_op jit(solution)/shard_map/relay/pallas_call | solution.py:458
  170.9 0.0 copy-start.1
  170.9 1.7 copy.14
  172.6 0.0 copy-done.1
  172.6 0.0 copy-start
  172.6 0.8 copy.15
  173.4 0.4 copy-done
  173.8 0.8 copy.16
Async XLA Ops:
  170.9 1.7 copy-start.1
  172.6 1.2 copy-start
